TPU v7x, 32 devices: a whole 2x2x4 slice. The times are simulated.
32 devices in a mesh: gx: 4 (over y, core), gy: 8 (over z, x).
Axes of the slice: x: 2, y: 2, z: 4, core: 2. Of those that a mesh axis runs over, the one named last changes fastest.
Arguments:
- x_block: float32 [16, 32, 64, 128], P(None, 'gx', 'gy'), may hold values from -8 to 8
- old_direction: float32 [16, 32, 64, 128], P(None, 'gx', 'gy'), may hold values from -6 to 6
- conductivity: float32 [32, 64, 128], P('gx', 'gy'), may hold values from 0.5 to 4
- fsai_diagonal: float32 [32, 64, 128], P('gx', 'gy'), may hold values from 0.2 to 0.6
- fsai_lower: float32 [13, 32, 64, 128], P(None, 'gx', 'gy'), may hold values from -0.9 to 0.9
- pattern: int32 [8, 13], replicated, may hold values 0 or 1
- step_size: float32 [16], replicated, may hold values from 0.3 to 1.5
- momentum: float32 [16], replicated, may hold values from 0.2 to 1
Outputs:
- x_next: float32 [16, 32, 64, 128], P(None, 'gx', 'gy')
- direction: float32 [16, 32, 64, 128], P(None, 'gx', 'gy')
- rayleigh: float32 [16, 16], replicated
All inputs are finite; a program needn't handle non-finite values.
Results may differ from a plain program's by a relative error of at most 0.00018.
Values sent between devices are 32-bit elements; how exact they have to be, the bound alone decides.
A program may use at most 64 MiB of HBM per device.

v0:
```python
import jax
import jax.numpy as jnp
from jax import lax
from jax.sharding import PartitionSpec as P

BLOCKS = 8


lower_offsets = [
    (a, b, c) for a in (-1, 0, 1) for b in (-1, 0, 1) for c in (-1, 0, 1) if (a, b, c) < (0, 0, 0)
]
face_offsets = [(1, 0, 0), (-1, 0, 0), (0, 1, 0), (0, -1, 0), (0, 0, 1), (0, 0, -1)]


def extended(cells, sides, width):
    for axis, dim in sides:
        count = lax.axis_size(axis)
        ends = count - 1
        head = lax.slice_in_dim(cells, 0, width, axis=dim)
        tail = lax.slice_in_dim(cells, cells.shape[dim] - width, cells.shape[dim], axis=dim)
        cells = jnp.concatenate(
            [
                lax.ppermute(tail, axis, [(i, (i + 1) % count) for i in range(ends)]),
                cells,
                lax.ppermute(head, axis, [((i + 1) % count, i) for i in range(ends)]),
            ],
            axis=dim,
        )
    return cells


def passed_along(array, axis, by):
    size = lax.axis_size(axis)
    pairs = [(i, i + by) for i in range(size) if 0 <= i + by < size]
    return lax.ppermute(array, axis, pairs)


def window(padded, step_x, step_y, step_z, region):
    size_x, size_y, size_z = region
    return padded[
        ...,
        1 + step_x : 1 + step_x + size_x,
        1 + step_y : 1 + step_y + size_y,
        1 + step_z : 1 + step_z + size_z,
    ]


def apply_stiffness(padded, kappa_pad, region):
    centre = window(padded, 0, 0, 0, region)
    kappa_here = window(kappa_pad, 0, 0, 0, region)
    summed = jnp.zeros(centre.shape, jnp.float32)
    for step_x, step_y, step_z in face_offsets:
        face = 0.5 * (kappa_here + window(kappa_pad, step_x, step_y, step_z, region))
        summed = summed + face * (centre - window(padded, step_x, step_y, step_z, region))
    return summed


def apply_factor(padded, diag_here, lower_here, region):
    summed = diag_here * window(padded, 0, 0, 0, region)
    for index, (step_x, step_y, step_z) in enumerate(lower_offsets):
        summed = summed + lower_here[index] * window(padded, step_x, step_y, step_z, region)
    return summed


def apply_transpose(padded, diag_pad, lower_pad, region):
    summed = window(diag_pad, 0, 0, 0, region) * window(padded, 0, 0, 0, region)
    for index, (step_x, step_y, step_z) in enumerate(lower_offsets):
        summed = summed + window(lower_pad[index], -step_x, -step_y, -step_z, region) * window(
            padded, -step_x, -step_y, -step_z, region
        )
    return summed


def pad_depth(field):
    widths = [(0, 0)] * (field.ndim - 1) + [(1, 1)]
    return jnp.pad(field, widths)


def quotient_of(x_block, image, scale):
    local_xx = jnp.sum(x_block * x_block, axis=(1, 2, 3))
    local_xa = jnp.sum(x_block * image, axis=(1, 2, 3))
    sum_xx, sum_xa = lax.psum((local_xx, local_xa), ("gx", "gy"))
    return sum_xa * scale / (sum_xx * scale + 1e-06)


def per_device(
    x_block, old_direction, conductivity, fsai_diagonal, fsai_lower, pattern, step_size, momentum
):
    size_x = x_block.shape[1]
    size_y = x_block.shape[2]
    size_z = x_block.shape[3]
    region = (size_x, size_y, size_z)
    vectors = x_block.shape[0]
    cell_count = size_x * size_y * size_z * lax.axis_size("gx") * lax.axis_size("gy")
    scale = 1.0 / cell_count
    block_id = jnp.arange(size_z, dtype=jnp.int32) // (size_z // BLOCKS)
    onehot = (block_id[:, None] == jnp.arange(BLOCKS, dtype=jnp.int32)[None, :]).astype(jnp.float32)
    active = jnp.dot(onehot, pattern.astype(jnp.float32), precision=lax.Precision.HIGHEST)
    lower_terms = fsai_lower * jnp.transpose(active)[:, None, None, :]
    fields = jnp.concatenate([conductivity[None], fsai_diagonal[None], lower_terms], axis=0)
    fields_wide = extended(fields, (("gx", 1), ("gy", 2)), 1)
    block_wide = pad_depth(extended(x_block, (("gx", 1), ("gy", 2)), 1))
    fields_pad = pad_depth(fields_wide)
    kappa_pad = fields_pad[0]
    diag_pad = fields_pad[1]
    lower_pad = fields_pad[2:]
    image = apply_stiffness(block_wide, kappa_pad, region)
    quotient = quotient_of(x_block, image, scale)
    gradient = image - quotient[:, None, None, None] * x_block
    near_pad = pad_depth(extended(gradient, (("gx", 1), ("gy", 2)), 1))
    product = apply_factor(near_pad, fsai_diagonal, lower_terms, region)
    side_wide = extended(product, (("gy", 2),), 1)
    upper_plane = passed_along(side_wide[:, :1], "gx", -1)
    lower_plane = jnp.zeros(upper_plane.shape, jnp.float32)
    product_pad = pad_depth(jnp.concatenate([lower_plane, side_wide, upper_plane], axis=1))
    smoothed = apply_transpose(product_pad, diag_pad, lower_pad, region)
    direction = smoothed + momentum[:, None, None, None] * old_direction
    direction_pad = pad_depth(extended(direction, (("gx", 1), ("gy", 2)), 1))
    direction_image = apply_stiffness(direction_pad, kappa_pad, region)
    advanced = x_block + step_size[:, None, None, None] * direction
    advanced_image = image + step_size[:, None, None, None] * direction_image
    local_gram = jnp.einsum("kxyz,jxyz->kj", advanced, advanced, precision=lax.Precision.HIGHEST)
    local_stiff = jnp.einsum(
        "kxyz,jxyz->kj", advanced, advanced_image, precision=lax.Precision.HIGHEST
    )
    gram_total, stiff_total = lax.psum((local_gram, local_stiff), ("gx", "gy"))
    identity = jnp.eye(vectors, dtype=jnp.float32)
    gram = gram_total * scale + 1e-05 * identity
    stiff = stiff_total * scale
    factor = jnp.linalg.cholesky(gram)
    inverse = jax.scipy.linalg.solve_triangular(factor, identity, lower=True)
    x_next = jnp.einsum("kj,jxyz->kxyz", inverse, advanced, precision=lax.Precision.HIGHEST)
    rayleigh = jnp.dot(
        jnp.dot(inverse, stiff, precision=lax.Precision.HIGHEST),
        jnp.transpose(inverse),
        precision=lax.Precision.HIGHEST,
    )
    return (x_next, direction, rayleigh)


def solution(mesh):
    placed = (
        P(None, "gx", "gy", None),
        P(None, "gx", "gy", None),
        P("gx", "gy", None),
        P("gx", "gy", None),
        P(None, "gx", "gy", None),
        P(),
        P(),
        P(),
    )
    return jax.shard_map(
        per_device,
        mesh=mesh,
        in_specs=placed,
        out_specs=(P(None, "gx", "gy", None), P(None, "gx", "gy", None), P()),
        check_vma=False,
    )
```

profile of v0, /device:TPU:0, one launch (start us, length us, event | category | flops | bytes accessed | tf_op | source)
XLA Modules:
  0.0 178.6 jit_solution(10476219828083600883)
XLA Ops:
  0.6 0.9 convolution_bitcast_fusion.2
  1.6 1.1 broadcast_multiply_fusion
  2.7 0.7 pad_maximum_fusion.38
  3.5 2.4 %collective-permute-start = (f32[15,1,8,128]{3,2,1,0:T(8,128)S(1)}, f32[15,1,8,128]{3,2,1,0:T(8,128)S(1)}, u32[]{:S(2)}, u32[]{:S(2)}) collective-permute-start(f32[15,1,8,128]{3,2,1,0:T(8,128)S(1)} %get-tuple-element.49), channel_id=1, source_target_pairs={{0,8},{8,16},{16,24},{1,9},{9,17},{17,25},{2,10},{10,18},{18,26},{... | collective-permute-start | bytes 184328 | tf_op jit(solution)/shard_map/ppermute | solution.py:23
  5.8 1.3 collective-permute-start.1
  7.1 0.3 copy.53
  7.5 5.2 %collective-permute-start.5 = (f32[16,1,8,128]{3,0,2,1:T(8,128)S(1)}, f32[16,1,8,128]{3,0,2,1:T(8,128)S(1)}, u32[]{:S(2)}, u32[]{:S(2)}) collective-permute-start(f32[16,1,8,128]{3,0,2,1:T(8,128)S(1)} %get-tuple-element.48), channel_id=1, source_target_pairs={{0,8},{8,16},{16,24},{1,9},{9,17},{17,25},{2,10},{10,18},{18,26},{... | collective-permute-start | bytes 196616 | tf_op jit(solution)/shard_map/ppermute | solution.py:23
  12.6 1.3 collective-permute-start.4
  13.9 0.2 multiply_reduce_fusion
  14.2 0.1 pad_maximum_fusion.35
  14.3 3.4 %collective-permute-start.2 = (f32[15,10,1,128]{3,0,2,1:T(8,128)S(1)}, f32[15,10,1,128]{3,0,2,1:T(8,128)S(1)}, u32[]{:S(2)}, u32[]{:S(2)}) collective-permute-start(f32[15,10,1,128]{3,0,2,1:T(8,128)S(1)} %copy.35), channel_id=1, source_target_pairs={{0,1},{1,2},{2,3},{3,4},{4,5},{5,6},{6,7},{8,9},{9,10},{10,11},{11... | collective-permute-start | bytes 230408 | tf_op jit(solution)/shard_map/ppermute | solution.py:23
  17.7 1.3 collective-permute-start.3
  19.1 0.3 constant_dynamic-update-slice_fusion.1
  19.4 1.3 collective-permute-start.6
  20.7 5.2 %collective-permute-start.7 = (f32[16,10,1,128]{3,0,2,1:T(8,128)S(1)}, f32[16,10,1,128]{3,0,2,1:T(8,128)S(1)}, u32[]{:S(2)}, u32[]{:S(2)}) collective-permute-start(f32[16,10,1,128]{3,0,2,1:T(8,128)S(1)} %get-tuple-element.37), channel_id=1, source_target_pairs={{0,1},{1,2},{2,3},{3,4},{4,5},{5,6},{6,7},{8,9},{9,10},{10,11},{11... | collective-permute-start | bytes 245768 | tf_op jit(solution)/shard_map/ppermute | solution.py:23
  25.9 0.1 copy.37
  26.0 0.1 copy.38
  26.1 2.8 %select_maximum_fusion = f32[15,10,10,130]{3,2,1,0:T(8,128)S(1)} fusion(f32[15,10,1,128]{3,2,1,0:T(1,128)S(1)} %copy.38, f32[15,10,1,128]{3,2,1,0:T(1,128)S(1)} %copy.37, f32[15,1,8,128]{3,2,1,0:T(8,128)S(1)} %collective-permute-done.1, f32[15,1,8,128]{3,2,1,0:T(8,128)S(1)} %collective-permute-done, f32[13,8,8,128]{3,2,1,0:T(8,128)S(1)} %broadcast_multiply_fusion, ...), kind=kLoop, calls=%fused_computation.13 | loop fusion | flops 3120000 | bytes 1548000 | tf_op jit(solution)/shard_map/concatenate | solution.py:21
  28.9 1.0 slice_bitcast_fusion.14
  29.9 0.1 fusion.95
  30.1 0.5 select_maximum_fusion.14
  30.6 0.8 multiply_reduce_fusion.1
  31.4 44.4 %all-reduce.6 = (f32[16]{0:T(128)S(1)}, f32[16]{0:T(128)S(1)}) all-reduce(f32[16]{0:T(128)S(1)} %multiply_reduce_fusion, f32[16]{0:T(128)S(1)} %get-tuple-element.16), channel_id=1, replica_groups=mesh['gx'=4,'gy'=8] {'gx','gy'}, use_global_device_ids=true, to_apply=%region_3.4 | all-reduce | flops 32 | bytes 256 | tf_op jit(solution)/shard_map/psum | solution.py:82
  75.8 0.3 multiply_subtract_fusion
  76.2 1.3 collective-permute-start.8
  77.5 1.3 collective-permute-start.9
  78.8 4.3 %collective-permute-done.9 = f32[16,1,8,128]{3,0,2,1:T(8,128)S(1)} collective-permute-done((f32[16,1,8,128]{3,0,2,1:T(8,128)S(1)}, f32[16,1,8,128]{3,0,2,1:T(8,128)S(1)}, u32[]{:S(2)}, u32[]{:S(2)}) %collective-permute-start.9) | collective-permute-done | bytes 65568 | tf_op jit(solution)/shard_map/ppermute | solution.py:25
  83.1 2.5 %collective-permute-start.10 = (f32[16,10,1,128]{3,0,2,1:T(8,128)S(1)}, f32[16,10,1,128]{3,0,2,1:T(8,128)S(1)}, u32[]{:S(2)}, u32[]{:S(2)}) collective-permute-start(f32[16,10,1,128]{3,0,2,1:T(8,128)S(1)} %get-tuple-element.35), channel_id=1, source_target_pairs={{0,1},{1,2},{2,3},{3,4},{4,5},{5,6},{6,7},{8,9},{9,10},{10,11},{11... | collective-permute-start | bytes 245768 | tf_op jit(solution)/shard_map/ppermute | solution.py:23
  85.7 1.3 collective-permute-start.11
  87.0 0.7 collective-permute-done.10
  87.8 4.3 %collective-permute-done.11 = f32[16,10,1,128]{3,0,2,1:T(8,128)S(1)} collective-permute-done((f32[16,10,1,128]{3,0,2,1:T(8,128)S(1)}, f32[16,10,1,128]{3,0,2,1:T(8,128)S(1)}, u32[]{:S(2)}, u32[]{:S(2)}) %collective-permute-start.11) | collective-permute-done | bytes 81952 | tf_op jit(solution)/shard_map/ppermute | solution.py:25
  92.1 0.5 select_maximum_fusion.10
  92.5 0.8 fusion.53
  93.4 3.9 %collective-permute-start.12 = (f32[16,8,1,128]{3,0,2,1:T(8,128)S(1)}, f32[16,8,1,128]{3,0,2,1:T(8,128)S(1)}, u32[]{:S(2)}, u32[]{:S(2)}) collective-permute-start(f32[16,8,1,128]{3,0,2,1:T(8,128)S(1)} %get-tuple-element.43), channel_id=1, source_target_pairs={{0,1},{1,2},{2,3},{3,4},{4,5},{5,6},{6,7},{8,9},{9,10},{10,11},{11... | collective-permute-start | bytes 196616 | tf_op jit(solution)/shard_map/ppermute | solution.py:23
  97.3 1.3 collective-permute-start.13
  98.6 0.7 collective-permute-done.12
  99.3 4.6 %collective-permute-done.13 = f32[16,8,1,128]{3,0,2,1:T(8,128)S(1)} collective-permute-done((f32[16,8,1,128]{3,0,2,1:T(8,128)S(1)}, f32[16,8,1,128]{3,0,2,1:T(8,128)S(1)}, u32[]{:S(2)}, u32[]{:S(2)}) %collective-permute-start.13) | collective-permute-done | bytes 65568 | tf_op jit(solution)/shard_map/ppermute | solution.py:25
  103.9 1.3 collective-permute-start.14
  105.2 1.0 slice.508
  106.2 1.0 slice.550
  107.3 0.1 slice.559
  107.6 0.1 slice.573
  107.9 0.1 pad_maximum_fusion
  108.1 0.6 copy-done.2
  108.7 1.3 fusion.16
  110.0 1.3 collective-permute-start.15
  111.3 4.5 %collective-permute-start.16 = (f32[16,1,8,128]{3,0,2,1:T(8,128)S(1)}, f32[16,1,8,128]{3,0,2,1:T(8,128)S(1)}, u32[]{:S(2)}, u32[]{:S(2)}) collective-permute-start(f32[16,1,8,128]{3,0,2,1:T(8,128)S(1)} %get-tuple-element.41), channel_id=1, source_target_pairs={{0,8},{8,16},{16,24},{1,9},{9,17},{17,25},{2,10},{10,18},{18,26},{... | collective-permute-start | bytes 196616 | tf_op jit(solution)/shard_map/ppermute | solution.py:23
  115.8 1.0 copy.56
  116.8 1.3 collective-permute-start.17
  118.1 4.9 %collective-permute-start.18 = (f32[16,10,1,128]{3,0,2,1:T(8,128)S(1)}, f32[16,10,1,128]{3,0,2,1:T(8,128)S(1)}, u32[]{:S(2)}, u32[]{:S(2)}) collective-permute-start(f32[16,10,1,128]{3,0,2,1:T(8,128)S(1)} %get-tuple-element.33), channel_id=1, source_target_pairs={{0,1},{1,2},{2,3},{3,4},{4,5},{5,6},{6,7},{8,9},{9,10},{10,11},{11... | collective-permute-start | bytes 245768 | tf_op jit(solution)/shard_map/ppermute | solution.py:23
  123.0 1.0 convolution_bitcast_fusion.1
  124.0 1.9 %collective-permute-done.18 = f32[16,10,1,128]{3,0,2,1:T(8,128)S(1)} collective-permute-done((f32[16,10,1,128]{3,0,2,1:T(8,128)S(1)}, f32[16,10,1,128]{3,0,2,1:T(8,128)S(1)}, u32[]{:S(2)}, u32[]{:S(2)}) %collective-permute-start.18) | collective-permute-done | bytes 81952 | tf_op jit(solution)/shard_map/ppermute | solution.py:23
  125.9 0.5 select_maximum_fusion.6
  126.5 1.4 convolution_bitcast_fusion
  127.8 43.8 %all-reduce.5 = (f32[16,16]{1,0:T(8,128)S(1)}, f32[16,16]{1,0:T(8,128)S(1)}) all-reduce(f32[16,16]{1,0:T(8,128)S(1)} %convolution_bitcast_fusion.1, f32[16,16]{1,0:T(8,128)S(1)} %convolution_bitcast_fusion), channel_id=1, replica_groups=mesh['gx'=4,'gy'=8] {'gx','gy'}, use_global_device_ids=true, to_apply=%region_4.5 | all-reduce | flops 512 | bytes 4096 | tf_op jit(solution)/shard_map/psum | solution.py:126
  171.7 1.5 cholesky.17
  173.2 0.6 compare_reduce_fusion
  173.8 0.6 fusion.97
  174.5 1.2 custom-call.7
  175.7 0.2 fusion.100
  175.9 0.9 fusion.98
  176.8 0.1 fusion.103
  176.9 0.7 fusion.118
  177.6 1.0 copy.55
  (80 shorter events, 1.0 us)
Async XLA Ops:
  0.6 6.5 %copy-start = (f32[16,8,8,128]{3,2,1,0:T(8,128)S(1)}, f32[16,8,8,128]{3,2,1,0:T(8,128)}, u32[]{:S(2)}) copy-start(f32[16,8,8,128]{3,2,1,0:T(8,128)} %param.8) | copy-start | bytes 1572868
  1.6 12.6 %copy-start.1 = (f32[8,8,128]{2,1,0:T(8,128)S(1)}, f32[8,8,128]{2,1,0:T(8,128)}, u32[]{:S(2)}) copy-start(f32[8,8,128]{2,1,0:T(8,128)} %param.11) | copy-start | bytes 98308
  1.6 12.6 %copy-start.3 = (f32[8,8,128]{2,1,0:T(8,128)S(1)}, f32[8,8,128]{2,1,0:T(8,128)}, u32[]{:S(2)}) copy-start(f32[8,8,128]{2,1,0:T(8,128)} %param.10) | copy-start | bytes 98308
  3.5 10.7 %collective-permute-start = (f32[15,1,8,128]{3,2,1,0:T(8,128)S(1)}, f32[15,1,8,128]{3,2,1,0:T(8,128)S(1)}, u32[]{:S(2)}, u32[]{:S(2)}) collective-permute-start(f32[15,1,8,128]{3,2,1,0:T(8,128)S(1)} %get-tuple-element.49), channel_id=1, source_target_pairs={{0,8},{8,16},{16,24},{1,9},{9,17},{17,25},{2,10},{10,18},{18,26},{... | collective-permute-start | bytes 184328 | tf_op jit(solution)/shard_map/ppermute | solution.py:23
  5.8 8.3 %collective-permute-start.1 = (f32[15,1,8,128]{3,2,1,0:T(8,128)S(1)}, f32[15,1,8,128]{3,2,1,0:T(8,128)S(1)}, u32[]{:S(2)}, u32[]{:S(2)}) collective-permute-start(f32[15,1,8,128]{3,2,1,0:T(8,128)S(1)} %get-tuple-element.50), channel_id=1, source_target_pairs={{8,0},{16,8},{24,16},{9,1},{17,9},{25,17},{10,2},{18,10},{26,18},{... | collective-permute-start | bytes 184328 | tf_op jit(solution)/shard_map/ppermute | solution.py:25
  7.5 11.6 %collective-permute-start.5 = (f32[16,1,8,128]{3,0,2,1:T(8,128)S(1)}, f32[16,1,8,128]{3,0,2,1:T(8,128)S(1)}, u32[]{:S(2)}, u32[]{:S(2)}) collective-permute-start(f32[16,1,8,128]{3,0,2,1:T(8,128)S(1)} %get-tuple-element.48), channel_id=1, source_target_pairs={{0,8},{8,16},{16,24},{1,9},{9,17},{17,25},{2,10},{10,18},{18,26},{... | collective-permute-start | bytes 196616 | tf_op jit(solution)/shard_map/ppermute | solution.py:23
  12.6 6.7 %collective-permute-start.4 = (f32[16,1,8,128]{3,0,2,1:T(8,128)S(1)}, f32[16,1,8,128]{3,0,2,1:T(8,128)S(1)}, u32[]{:S(2)}, u32[]{:S(2)}) collective-permute-start(f32[16,1,8,128]{3,0,2,1:T(8,128)S(1)} %get-tuple-element.47), channel_id=1, source_target_pairs={{8,0},{16,8},{24,16},{9,1},{17,9},{25,17},{10,2},{18,10},{26,18},{... | collective-permute-start | bytes 196616 | tf_op jit(solution)/shard_map/ppermute | solution.py:25
  14.3 11.6 %collective-permute-start.2 = (f32[15,10,1,128]{3,0,2,1:T(8,128)S(1)}, f32[15,10,1,128]{3,0,2,1:T(8,128)S(1)}, u32[]{:S(2)}, u32[]{:S(2)}) collective-permute-start(f32[15,10,1,128]{3,0,2,1:T(8,128)S(1)} %copy.35), channel_id=1, source_target_pairs={{0,1},{1,2},{2,3},{3,4},{4,5},{5,6},{6,7},{8,9},{9,10},{10,11},{11... | collective-permute-start | bytes 230408 | tf_op jit(solution)/shard_map/ppermute | solution.py:23
  17.7 8.3 %collective-permute-start.3 = (f32[15,10,1,128]{3,0,2,1:T(8,128)S(1)}, f32[15,10,1,128]{3,0,2,1:T(8,128)S(1)}, u32[]{:S(2)}, u32[]{:S(2)}) collective-permute-start(f32[15,10,1,128]{3,0,2,1:T(8,128)S(1)} %copy.36), channel_id=1, source_target_pairs={{1,0},{2,1},{3,2},{4,3},{5,4},{6,5},{7,6},{9,8},{10,9},{11,10},{12... | collective-permute-start | bytes 230408 | tf_op jit(solution)/shard_map/ppermute | solution.py:25
  19.4 10.7 %collective-permute-start.6 = (f32[16,10,1,128]{3,0,2,1:T(8,128)S(1)}, f32[16,10,1,128]{3,0,2,1:T(8,128)S(1)}, u32[]{:S(2)}, u32[]{:S(2)}) collective-permute-start(f32[16,10,1,128]{3,0,2,1:T(8,128)S(1)} %get-tuple-element.38), channel_id=1, source_target_pairs={{1,0},{2,1},{3,2},{4,3},{5,4},{6,5},{7,6},{9,8},{10,9},{11,10},{12... | collective-permute-start | bytes 245768 | tf_op jit(solution)/shard_map/ppermute | solution.py:25
  20.7 9.4 %collective-permute-start.7 = (f32[16,10,1,128]{3,0,2,1:T(8,128)S(1)}, f32[16,10,1,128]{3,0,2,1:T(8,128)S(1)}, u32[]{:S(2)}, u32[]{:S(2)}) collective-permute-start(f32[16,10,1,128]{3,0,2,1:T(8,128)S(1)} %get-tuple-element.37), channel_id=1, source_target_pairs={{0,1},{1,2},{2,3},{3,4},{4,5},{5,6},{6,7},{8,9},{9,10},{10,11},{11... | collective-permute-start | bytes 245768 | tf_op jit(solution)/shard_map/ppermute | solution.py:23
  30.0 1.4 copy-start.4
  30.0 1.3 copy-start.6
  30.1 1.3 copy-start.8
  30.1 1.3 copy-start.10
  30.1 1.3 copy-start.12
  30.1 1.3 copy-start.14
  76.2 2.6 %collective-permute-start.8 = (f32[16,1,8,128]{3,0,2,1:T(8,128)S(1)}, f32[16,1,8,128]{3,0,2,1:T(8,128)S(1)}, u32[]{:S(2)}, u32[]{:S(2)}) collective-permute-start(f32[16,1,8,128]{3,0,2,1:T(8,128)S(1)} %get-tuple-element.45), channel_id=1, source_target_pairs={{0,8},{8,16},{16,24},{1,9},{9,17},{17,25},{2,10},{10,18},{18,26},{... | collective-permute-start | bytes 196616 | tf_op jit(solution)/shard_map/ppermute | solution.py:23
  77.5 5.7 %collective-permute-start.9 = (f32[16,1,8,128]{3,0,2,1:T(8,128)S(1)}, f32[16,1,8,128]{3,0,2,1:T(8,128)S(1)}, u32[]{:S(2)}, u32[]{:S(2)}) collective-permute-start(f32[16,1,8,128]{3,0,2,1:T(8,128)S(1)} %get-tuple-element.46), channel_id=1, source_target_pairs={{8,0},{16,8},{24,16},{9,1},{17,9},{25,17},{10,2},{18,10},{26,18},{... | collective-permute-start | bytes 196616 | tf_op jit(solution)/shard_map/ppermute | solution.py:25
  83.1 4.6 %collective-permute-start.10 = (f32[16,10,1,128]{3,0,2,1:T(8,128)S(1)}, f32[16,10,1,128]{3,0,2,1:T(8,128)S(1)}, u32[]{:S(2)}, u32[]{:S(2)}) collective-permute-start(f32[16,10,1,128]{3,0,2,1:T(8,128)S(1)} %get-tuple-element.35), channel_id=1, source_target_pairs={{0,1},{1,2},{2,3},{3,4},{4,5},{5,6},{6,7},{8,9},{9,10},{10,11},{11... | collective-permute-start | bytes 245768 | tf_op jit(solution)/shard_map/ppermute | solution.py:23
  85.7 6.3 %collective-permute-start.11 = (f32[16,10,1,128]{3,0,2,1:T(8,128)S(1)}, f32[16,10,1,128]{3,0,2,1:T(8,128)S(1)}, u32[]{:S(2)}, u32[]{:S(2)}) collective-permute-start(f32[16,10,1,128]{3,0,2,1:T(8,128)S(1)} %get-tuple-element.36), channel_id=1, source_target_pairs={{1,0},{2,1},{3,2},{4,3},{5,4},{6,5},{7,6},{9,8},{10,9},{11,10},{12... | collective-permute-start | bytes 245768 | tf_op jit(solution)/shard_map/ppermute | solution.py:25
  93.4 5.9 %collective-permute-start.12 = (f32[16,8,1,128]{3,0,2,1:T(8,128)S(1)}, f32[16,8,1,128]{3,0,2,1:T(8,128)S(1)}, u32[]{:S(2)}, u32[]{:S(2)}) collective-permute-start(f32[16,8,1,128]{3,0,2,1:T(8,128)S(1)} %get-tuple-element.43), channel_id=1, source_target_pairs={{0,1},{1,2},{2,3},{3,4},{4,5},{5,6},{6,7},{8,9},{9,10},{10,11},{11... | collective-permute-start | bytes 196616 | tf_op jit(solution)/shard_map/ppermute | solution.py:23
  97.3 6.6 %collective-permute-start.13 = (f32[16,8,1,128]{3,0,2,1:T(8,128)S(1)}, f32[16,8,1,128]{3,0,2,1:T(8,128)S(1)}, u32[]{:S(2)}, u32[]{:S(2)}) collective-permute-start(f32[16,8,1,128]{3,0,2,1:T(8,128)S(1)} %get-tuple-element.44), channel_id=1, source_target_pairs={{1,0},{2,1},{3,2},{4,3},{5,4},{6,5},{7,6},{9,8},{10,9},{11,10},{12... | collective-permute-start | bytes 196616 | tf_op jit(solution)/shard_map/ppermute | solution.py:25
  103.9 4.0 %collective-permute-start.14 = (f32[16,1,10,128]{3,0,2,1:T(8,128)S(1)}, f32[16,1,10,128]{3,0,2,1:T(8,128)S(1)}, u32[]{:S(2)}, u32[]{:S(2)}) collective-permute-start(f32[16,1,10,128]{3,0,2,1:T(8,128)S(1)} %pad_maximum_fusion.26), channel_id=1, source_target_pairs={{8,0},{16,8},{24,16},{9,1},{17,9},{25,17},{10,2},{18,10},{26,18},{... | collective-permute-start | bytes 245768 | tf_op jit(solution)/shard_map/ppermute | solution.py:35
  107.6 1.0 copy-start.2
  107.6 1.0 copy-start.17
  110.0 13.0 %copy-start.16 = (f32[16]{0:T(128)S(1)}, f32[16]{0:T(128)}, u32[]{:S(2)}) copy-start(f32[16]{0:T(128)} %param.14) | copy-start | bytes 196
  110.0 6.7 %collective-permute-start.15 = (f32[16,1,8,128]{3,0,2,1:T(8,128)S(1)}, f32[16,1,8,128]{3,0,2,1:T(8,128)S(1)}, u32[]{:S(2)}, u32[]{:S(2)}) collective-permute-start(f32[16,1,8,128]{3,0,2,1:T(8,128)S(1)} %get-tuple-element.42), channel_id=1, source_target_pairs={{8,0},{16,8},{24,16},{9,1},{17,9},{25,17},{10,2},{18,10},{26,18},{... | collective-permute-start | bytes 196616 | tf_op jit(solution)/shard_map/ppermute | solution.py:25
  111.3 5.4 %collective-permute-start.16 = (f32[16,1,8,128]{3,0,2,1:T(8,128)S(1)}, f32[16,1,8,128]{3,0,2,1:T(8,128)S(1)}, u32[]{:S(2)}, u32[]{:S(2)}) collective-permute-start(f32[16,1,8,128]{3,0,2,1:T(8,128)S(1)} %get-tuple-element.41), channel_id=1, source_target_pairs={{0,8},{8,16},{16,24},{1,9},{9,17},{17,25},{2,10},{10,18},{18,26},{... | collective-permute-start | bytes 196616 | tf_op jit(solution)/shard_map/ppermute | solution.py:23
  116.8 7.2 %collective-permute-start.17 = (f32[16,10,1,128]{3,0,2,1:T(8,128)S(1)}, f32[16,10,1,128]{3,0,2,1:T(8,128)S(1)}, u32[]{:S(2)}, u32[]{:S(2)}) collective-permute-start(f32[16,10,1,128]{3,0,2,1:T(8,128)S(1)} %get-tuple-element.34), channel_id=1, source_target_pairs={{1,0},{2,1},{3,2},{4,3},{5,4},{6,5},{7,6},{9,8},{10,9},{11,10},{12... | collective-permute-start | bytes 245768 | tf_op jit(solution)/shard_map/ppermute | solution.py:25
  118.1 8.3 %copy-start.5 = (f32[8,8,128]{2,1,0:T(8,128)S(1)}, f32[8,8,128]{2,1,0:T(8,128)}, u32[]{:S(2)}) copy-start(f32[8,8,128]{2,1,0:T(8,128)} %copy-done.4) | copy-start | bytes 98308
  118.1 8.3 %copy-start.7 = (f32[8,8,128]{2,1,0:T(8,128)S(1)}, f32[8,8,128]{2,1,0:T(8,128)}, u32[]{:S(2)}) copy-start(f32[8,8,128]{2,1,0:T(8,128)} %copy-done.6) | copy-start | bytes 98308
  118.1 8.3 %copy-start.9 = (f32[8,8,128]{2,1,0:T(8,128)S(1)}, f32[8,8,128]{2,1,0:T(8,128)}, u32[]{:S(2)}) copy-start(f32[8,8,128]{2,1,0:T(8,128)} %copy-done.8) | copy-start | bytes 98308
  118.1 8.3 %copy-start.11 = (f32[8,8,128]{2,1,0:T(8,128)S(1)}, f32[8,8,128]{2,1,0:T(8,128)}, u32[]{:S(2)}) copy-start(f32[8,8,128]{2,1,0:T(8,128)} %copy-done.10) | copy-start | bytes 98308
  118.1 8.3 %copy-start.13 = (f32[8,8,128]{2,1,0:T(8,128)S(1)}, f32[8,8,128]{2,1,0:T(8,128)}, u32[]{:S(2)}) copy-start(f32[8,8,128]{2,1,0:T(8,128)} %copy-done.12) | copy-start | bytes 98308
  118.1 8.3 %copy-start.15 = (f32[8,8,128]{2,1,0:T(8,128)S(1)}, f32[8,8,128]{2,1,0:T(8,128)}, u32[]{:S(2)}) copy-start(f32[8,8,128]{2,1,0:T(8,128)} %copy-done.14) | copy-start | bytes 98308
  118.1 7.8 %collective-permute-start.18 = (f32[16,10,1,128]{3,0,2,1:T(8,128)S(1)}, f32[16,10,1,128]{3,0,2,1:T(8,128)S(1)}, u32[]{:S(2)}, u32[]{:S(2)}) collective-permute-start(f32[16,10,1,128]{3,0,2,1:T(8,128)S(1)} %get-tuple-element.33), channel_id=1, source_target_pairs={{0,1},{1,2},{2,3},{3,4},{4,5},{5,6},{6,7},{8,9},{9,10},{10,11},{11... | collective-permute-start | bytes 245768 | tf_op jit(solution)/shard_map/ppermute | solution.py:23
where the time goes:
time: 180 us; the launch traced here: 179 us
  blocking collectives  88.1 us (49%)
  starting transfers between devices  46.1 us (26%)
  waiting for transfers between devices  16.5 us (9%)
  other arithmetic  14 us (8%)
  local copies, waits for them, and re-layouts  7.16 us (4%)
  matrix products  5.21 us (3%)
    psum x1, blocking collectives, quotient_of(): sum_xx, sum_xa = lax.psum((local_xx, local_xa), ('gx', 'gy'))  44.4 us
    psum x1, blocking collectives, per_device(): gram_total, stiff_total = lax.psum((local_gram, local_stiff), ('gx', 'gy'))  43.8 us
    ppermute x9, starting transfers between devices, extended(): lax.ppermute(tail, axis, [(i, (i + 1) % count) for i in range(ends)])  33.2 us
    ppermute x9, waiting for transfers between devices, extended(): lax.ppermute(head, axis, [((i + 1) % count, i) for i in range(ends)])  13.2 us
    ppermute x9, starting transfers between devices, extended(): lax.ppermute(head, axis, [((i + 1) % count, i) for i in range(ends)])  11.6 us
    concatenate x7, other arithmetic, extended(): jnp.concatenate([lax.ppermute(tail, axis, [(i, (i + 1) % count) for i in...  4.35 us
  transfers between devices with their start and end apart: 19, of which 6 were waited for; matrix products, arithmetic and copies ran while one was open for 5% of the time, Pallas kernels for 0%

commit v1 on v0

v1 whole, which is shorter than its diff:
```python
import functools

import jax
import jax.numpy as jnp
from jax import lax
from jax.experimental import pallas as pl
from jax.experimental.pallas import tpu as pltpu
from jax.sharding import PartitionSpec as P

MESH = pl.DeviceIdType.MESH
F32 = jnp.float32
BF16 = jnp.bfloat16

lower_offsets = [
    (a, b, c) for a in (-1, 0, 1) for b in (-1, 0, 1) for c in (-1, 0, 1) if (a, b, c) < (0, 0, 0)
]
DIAG = len(lower_offsets)
SIDES = [(1, 0), (-1, 0), (0, 1), (0, -1)]


def split3(value):
    high = value.astype(BF16)
    rest = value - high.astype(F32)
    middle = rest.astype(BF16)
    low = (rest - middle.astype(F32)).astype(BF16)
    return high, middle, low


def kernel(
    nx, ny, scale,
    x_in, old_in, cond_in, diag_in, lower_in, pattern_in, step_in, mom_in,
    next_out, dir_out, ray_out,
    xs, im, gr, pr, pt, adv,
    recv_x, recv_y0, recv_y1, recv_c, halo_x, halo_y,
    k_side, k_stage, coef, lm, lp,
    ab, abh, q_x, q_y, g_x, g_y,
    send_sem, recv_sem, send_x, recv_gx, send_y, recv_gy,
):
    ix, iy = lax.axis_index("gx"), lax.axis_index("gy")
    size_x, size_y = cond_in.shape[0], cond_in.shape[1]
    depth = cond_in.shape[2]
    vectors = xs.shape[2]
    cells = size_x * size_y
    blocks = pattern_in.shape[0]
    zero_col = jnp.zeros((vectors, depth), F32)
    zero_tile = jnp.zeros((size_y, depth), F32)

    def exists(sx, sy):
        found = None
        for ok, step in (
            (ix + 1 < nx, sx > 0), (ix > 0, sx < 0), (iy + 1 < ny, sy > 0), (iy > 0, sy < 0)
        ):
            if step:
                found = ok if found is None else jnp.logical_and(found, ok)
        return found

    def copy_of(item):
        src, dst, sx, sy, slot = item
        return pltpu.make_async_remote_copy(
            src_ref=src, dst_ref=dst, send_sem=send_sem.at[slot], recv_sem=recv_sem.at[slot],
            device_id=(ix + sx, iy + sy), device_id_type=MESH,
        )

    def start(items):
        for item in items:
            @pl.when(exists(item[2], item[3]))
            def _(item=item):
                copy_of(item).start()

    def wait_recv(items):
        for item in items:
            @pl.when(exists(-item[2], -item[3]))
            def _(item=item):
                copy_of(item).wait_recv()

    def wait_send(items):
        for item in items:
            @pl.when(exists(item[2], item[3]))
            def _(item=item):
                copy_of(item).wait_send()

    def group_start(buf, turn, n, me, place, sends, recvs):
        for s in range(1, n):
            peer = lax.rem(me + s, n)
            pltpu.make_async_remote_copy(
                src_ref=buf.at[me], dst_ref=buf.at[me], send_sem=sends.at[turn, s],
                recv_sem=recvs.at[turn, s], device_id=place(peer), device_id_type=MESH,
            ).start()

    def group_wait(buf, turn, n, me, place, sends, recvs):
        for s in range(1, n):
            peer = lax.rem(me + n - s, n)
            pltpu.make_async_remote_copy(
                src_ref=buf.at[peer], dst_ref=buf.at[peer], send_sem=sends.at[turn, s],
                recv_sem=recvs.at[turn, s], device_id=place(peer), device_id_type=MESH,
            ).wait()

    def along_x(peer):
        return (peer, iy)

    def along_y(peer):
        return (ix, peer)

    def reduce_start(buf_x, turn, tile):
        buf_x[ix] = tile
        group_start(buf_x, turn, nx, ix, along_x, send_x, recv_gx)

    def reduce_finish(buf_x, buf_y, turn):
        group_wait(buf_x, turn, nx, ix, along_x, send_x, recv_gx)
        total = buf_x[0]
        for i in range(1, nx):
            total = total + buf_x[i]
        buf_y[iy] = total
        group_start(buf_y, turn, ny, iy, along_y, send_y, recv_gy)
        group_wait(buf_y, turn, ny, iy, along_y, send_y, recv_gy)
        total = buf_y[0]
        for i in range(1, ny):
            total = total + buf_y[i]
        return total

    for buf in (xs, im):
        for y in range(size_y + 2):
            buf[0, y] = zero_col
            buf[size_x + 1, y] = zero_col
        for x in range(1, size_x + 1):
            buf[x, 0] = zero_col
            buf[x, size_y + 1] = zero_col
    for i in range(4):
        k_side[i] = zero_tile
    for i in range(size_y):
        recv_x[i] = zero_col
        halo_x[i] = zero_col
    for i in range(size_x):
        recv_y0[i] = zero_col
        recv_y1[i] = zero_col
        halo_y[i] = zero_col
    recv_c[0] = zero_col
    recv_c[1] = zero_col

    barrier = pltpu.get_barrier_semaphore()
    for s in range(1, nx):
        pl.semaphore_signal(barrier, inc=1, device_id=along_x(lax.rem(ix + s, nx)), device_id_type=MESH)
    for s in range(1, ny):
        pl.semaphore_signal(barrier, inc=1, device_id=along_y(lax.rem(iy + s, ny)), device_id_type=MESH)
    diagonal = 0
    for sx in (-1, 1):
        for sy in (-1, 1):
            there = exists(sx, sy)
            diagonal = diagonal + jnp.where(there, 1, 0)

            @pl.when(there)
            def _(sx=sx, sy=sy):
                pl.semaphore_signal(barrier, inc=1, device_id=(ix + sx, iy + sy), device_id_type=MESH)

    def turn_in(x, _):
        for y in range(size_y):
            xs[x + 1, y + 1] = x_in[pl.ds(x * size_y + y, vectors, stride=cells), :]
        return 0

    lax.fori_loop(0, size_x, turn_in, 0)
    k_stage[0] = cond_in[:, size_y - 1, :]
    k_stage[1] = cond_in[:, 0, :]

    pl.semaphore_wait(barrier, nx - 1 + ny - 1 + diagonal)

    inner_x, inner_y = pl.ds(1, size_x), pl.ds(1, size_y)
    first = [
        (k_stage.at[0], k_side.at[2], 0, 1, 0),
        (k_stage.at[1], k_side.at[3], 0, -1, 1),
        (cond_in.at[size_x - 1], k_side.at[0], 1, 0, 2),
        (cond_in.at[0], k_side.at[1], -1, 0, 3),
        (xs.at[inner_x, size_y], xs.at[inner_x, 0], 0, 1, 4),
        (xs.at[inner_x, 1], xs.at[inner_x, size_y + 1], 0, -1, 5),
        (xs.at[size_x, inner_y], xs.at[0, inner_y], 1, 0, 6),
        (xs.at[1, inner_y], xs.at[size_x + 1, inner_y], -1, 0, 7),
        (xs.at[size_x, size_y], xs.at[0, 0], 1, 1, 8),
        (xs.at[size_x, 1], xs.at[0, size_y + 1], 1, -1, 9),
    ]
    start(first)

    lane = lax.broadcasted_iota(jnp.int32, (size_y, depth), 1)
    piece = lane // (depth // blocks)
    for o in range(DIAG):
        dz = lower_offsets[o][2]
        keep = jnp.zeros((size_y, depth), F32)
        for b in range(blocks):
            keep = jnp.where(piece == b, pattern_in[b, o].astype(F32), keep)
        if dz:
            keep = jnp.where(lane == (0 if dz < 0 else depth - 1), 0.0, keep)

        def fill(x, _, o=o, dz=dz, keep=keep):
            term = lower_in[o, x] * keep
            lm[o, x + 1, pl.ds(2, size_y), :] = term
            lp[o, x] = pltpu.roll(term, dz % depth, 1) if dz else term
            return 0

        lax.fori_loop(0, size_x, fill, 0)

    def fill_diag(x, _):
        lm[DIAG, x + 1, pl.ds(2, size_y), :] = diag_in[x]
        return 0

    lax.fori_loop(0, size_x, fill_diag, 0)

    def rims(o, _):
        for x in range(size_x + 2):
            if x in (0, size_x + 1):
                lm[o, x] = jnp.zeros((lm.shape[2], depth), F32)
            else:
                lm[o, x, pl.ds(0, 2), :] = jnp.zeros((2, depth), F32)
                lm[o, x, pl.ds(size_y + 2, 2), :] = jnp.zeros((2, depth), F32)
        return 0

    lax.fori_loop(0, DIAG + 1, rims, 0)
    for y in range(size_y + 4):
        pr[0, y] = zero_col
        pr[size_x + 1, y] = zero_col
    for x in range(1, size_x + 1):
        for y in (0, 1, size_y + 2, size_y + 3):
            pr[x, y] = zero_col
    for y in range(size_y + 2):
        adv[0, y] = zero_col
        adv[size_x + 1, y] = zero_col
    for x in range(1, size_x + 1):
        adv[x, 0] = zero_col
        adv[x, size_y + 1] = zero_col

    row = lax.broadcasted_iota(jnp.int32, (vectors, depth), 0)
    step_col, mom_col = zero_col, zero_col
    for k in range(vectors):
        step_col = jnp.where(row == k, step_in[k], step_col)
        mom_col = jnp.where(row == k, mom_in[k], mom_col)

    wait_recv(first[:4])
    row8 = lax.broadcasted_iota(jnp.int32, (size_y, depth), 0)

    def faces(x, _):
        here = cond_in[x]
        below = jnp.where(x == 0, k_side[0], cond_in[jnp.maximum(x - 1, 0)])
        above = jnp.where(x == size_x - 1, k_side[1], cond_in[jnp.minimum(x + 1, size_x - 1)])
        left = jnp.where(row8 == 0, k_side[2, pl.ds(x, 1), :], pltpu.roll(here, 1, 0))
        right = jnp.where(row8 == size_y - 1, k_side[3, pl.ds(x, 1), :], pltpu.roll(here, size_y - 1, 0))
        back = jnp.where(lane == 0, 0.0, pltpu.roll(here, 1, 1))
        front = jnp.where(lane == depth - 1, 0.0, pltpu.roll(here, depth - 1, 1))
        total = None
        for i, near in enumerate((below, above, left, right, back, front)):
            face = 0.5 * (here + near)
            total = face if total is None else total + face
            if i == 4:
                face = jnp.where(lane == 0, 0.0, face)
            if i == 5:
                face = jnp.where(lane == depth - 1, 0.0, face)
            coef[i + 1, x] = face
        coef[0, x] = total
        return 0

    lax.fori_loop(0, size_x, faces, 0)

    def stiffness(buf, x, y):
        centre = buf[x + 1, y + 1]

        def c(i):
            return coef[i, x, pl.ds(y, 1), :]

        return (
            c(0) * centre
            - c(1) * buf[x, y + 1] - c(2) * buf[x + 2, y + 1]
            - c(3) * buf[x + 1, y] - c(4) * buf[x + 1, y + 2]
            - c(5) * pltpu.roll(centre, 1, 1) - c(6) * pltpu.roll(centre, depth - 1, 1)
        )

    wait_recv(first[4:])

    def images(x, sums):
        sum_xx, sum_xa = sums
        for y in range(size_y):
            centre = xs[x + 1, y + 1]
            image = stiffness(xs, x, y)
            im[x + 1, y + 1] = image
            sum_xx = sum_xx + centre * centre
            sum_xa = sum_xa + centre * image
        return sum_xx, sum_xa

    sum_xx, sum_xa = lax.fori_loop(0, size_x, images, (zero_col, zero_col))
    lane16 = lax.broadcasted_iota(jnp.int32, (vectors, depth), 1)
    both = jnp.where(
        lane16 < depth // 2,
        jnp.sum(sum_xx, axis=1, keepdims=True), jnp.sum(sum_xa, axis=1, keepdims=True),
    )
    reduce_start(q_x, 0, both)
    second = [
        (im.at[inner_x, size_y], im.at[inner_x, 0], 0, 1, 10),
        (im.at[inner_x, 1], im.at[inner_x, size_y + 1], 0, -1, 11),
        (im.at[size_x, inner_y], im.at[0, inner_y], 1, 0, 12),
        (im.at[size_x, size_y], im.at[0, 0], 1, 1, 13),
        (im.at[size_x, 1], im.at[0, size_y + 1], 1, -1, 14),
    ]
    start(second)
    both = reduce_finish(q_x, q_y, 0)
    quotient = both[:, depth // 2 : depth // 2 + 1] * scale / (both[:, 0:1] * scale + 1e-06)
    quotient = jnp.broadcast_to(quotient, (vectors, depth))
    wait_recv(second)

    def gradients(x, _):
        for y in range(size_y + 2):
            gr[x, y] = im[x, y] - quotient * xs[x, y]
        return 0

    lax.fori_loop(0, size_x + 1, gradients, 0)

    def products(x, _):
        for y in range(size_y):
            parts = {0: diag_in[x, pl.ds(y, 1), :] * gr[x + 1, y + 1], -1: zero_col, 1: zero_col}
            for o, (dx, dy, dz) in enumerate(lower_offsets):
                parts[dz] = parts[dz] + lp[o, x, pl.ds(y, 1), :] * gr[x + 1 + dx, y + 1 + dy]
            pr[x + 1, y + 2] = (
                parts[0] + pltpu.roll(parts[-1], 1, 1) + pltpu.roll(parts[1], depth - 1, 1)
            )
        return 0

    lax.fori_loop(0, size_x, products, 0)

    def target(x, y):
        parts = {0: lm[DIAG, x, pl.ds(y + 1, 1), :] * pr[x, y + 1], -1: zero_col, 1: zero_col}
        for o, (dx, dy, dz) in enumerate(lower_offsets):
            parts[dz] = parts[dz] + lm[o, x - dx, pl.ds(y + 1 - dy, 1), :] * pr[x - dx, y + 1 - dy]
        pt[x, y] = parts[0] + pltpu.roll(parts[-1], depth - 1, 1) + pltpu.roll(parts[1], 1, 1)

    for y in range(size_y + 2):
        target(0, y)

    def rim_targets(x, _):
        target(x, 0)
        target(x, size_y + 1)
        return 0

    lax.fori_loop(1, size_x + 1, rim_targets, 0)
    third = [
        (pt.at[inner_x, 0], recv_y0, 0, -1, 15),
        (pt.at[inner_x, size_y + 1], recv_y1, 0, 1, 16),
        (pt.at[0, inner_y], recv_x, -1, 0, 17),
        (pt.at[0, 0], recv_c.at[0], -1, -1, 18),
        (pt.at[0, size_y + 1], recv_c.at[1], -1, 1, 19),
    ]
    start(third)

    def own_targets(x, _):
        for y in range(1, size_y + 1):
            target(x, y)
        return 0

    lax.fori_loop(1, size_x + 1, own_targets, 0)
    wait_recv(third)
    for y in range(size_y):
        pt[size_x, y + 1] = pt[size_x, y + 1] + recv_x[y]
    for x in range(size_x):
        pt[x + 1, size_y] = pt[x + 1, size_y] + recv_y0[x]
        pt[x + 1, 1] = pt[x + 1, 1] + recv_y1[x]
    pt[size_x, size_y] = pt[size_x, size_y] + recv_c[0]
    pt[size_x, 1] = pt[size_x, 1] + recv_c[1]

    def at_column(index):
        return pl.ds(pl.multiple_of(index * depth, depth), depth)

    def put(buf, base, index, value):
        for i, part in enumerate(split3(value)):
            buf[base + i * vectors : base + (i + 1) * vectors, at_column(index)] = part

    def advance(x, _):
        for y in range(size_y):
            spot = pl.ds(x * size_y + y, vectors, stride=cells)
            direction = pt[x + 1, y + 1] + mom_col * old_in[spot, :]
            dir_out[spot, :] = direction
            advanced = xs[x + 1, y + 1] + step_col * direction
            adv[x + 1, y + 1] = advanced
            put(ab, 0, x * size_y + y, advanced)
        return 0

    lax.fori_loop(0, size_x, advance, 0)
    fourth = [
        (adv.at[inner_x, 1], halo_y, 0, -1, 20),
        (adv.at[1, inner_y], halo_x, -1, 0, 21),
    ]
    start(fourth)

    def advanced_images(x, _):
        for y in range(size_y):
            put(ab, 3 * vectors, x * size_y + y, stiffness(adv, x, y))
        return 0

    lax.fori_loop(0, size_x, advanced_images, 0)
    nt = (((1,), (1,)), ((), ()))
    grams = lax.dot_general(ab[0 : 3 * vectors, :], ab[...], nt, preferred_element_type=F32)
    wait_recv(fourth)
    for y in range(size_y):
        put(abh, 0, y, adv[size_x, y + 1])
        put(abh, 3 * vectors, y, -coef[2, size_x - 1, pl.ds(y, 1), :] * halo_x[y])
    for x in range(size_x):
        put(abh, 0, size_y + x, adv[x + 1, size_y])
        put(abh, 3 * vectors, size_y + x, -coef[4, x, pl.ds(size_y - 1, 1), :] * halo_y[x])
    crossed = lax.dot_general(abh[...], abh[...], nt, preferred_element_type=F32)

    def rows(array, base):
        return (
            array[base : base + vectors]
            + array[base + vectors : base + 2 * vectors]
            + array[base + 2 * vectors : base + 3 * vectors]
        )

    def wide(array):
        return jnp.concatenate([array, jnp.zeros((vectors, depth - 6 * vectors), F32)], axis=1)

    def lanes(array):
        return (
            array + pltpu.roll(array, depth - vectors, 1) + pltpu.roll(array, depth - 2 * vectors, 1)
        )

    main = lanes(wide(rows(grams, 0)))
    upper = lanes(wide(rows(crossed, 0)))
    lower = lanes(wide(rows(crossed, 3 * vectors)))
    stiff = pltpu.roll(main + upper, depth - 2 * vectors, 1) + pltpu.roll(lower, vectors, 1)
    packed = jnp.where(lane16 < vectors, main, jnp.where(lane16 < 2 * vectors, stiff, 0.0))
    reduce_start(g_x, 1, packed)
    packed = reduce_finish(g_x, g_y, 1) * scale

    aug = packed + jnp.where(row == lane16, 1e-05, 0.0)
    aug = aug + jnp.where(row + 2 * vectors == lane16, 1.0, 0.0)
    for j in range(vectors - 1):
        ratio = aug[:, j : j + 1] / aug[j : j + 1, j : j + 1]
        aug = aug - jnp.where(row > j, ratio * aug[j : j + 1, :], 0.0)
    pivots = jnp.sum(jnp.where(row == lane16, aug, 0.0), axis=1, keepdims=True)
    aug = aug / jnp.sqrt(pivots)
    inverse = aug[:, 2 * vectors : 3 * vectors]
    ray_out[...] = lax.dot_general(
        aug[:, vectors : 2 * vectors], inverse, nt,
        preferred_element_type=F32, precision=lax.Precision.HIGHEST,
    )
    weights = jnp.concatenate(
        [jnp.concatenate([part.astype(F32)] * 3, axis=1) for part in split3(inverse)], axis=0
    ).astype(BF16)

    def rotate(x, _):
        wide_part = pl.ds(pl.multiple_of(x * size_y * depth, depth), size_y * depth)
        mixed = rows(
            jnp.dot(weights, ab[0 : 3 * vectors, wide_part], preferred_element_type=F32), 0
        )
        for y in range(size_y):
            next_out[pl.ds(x * size_y + y, vectors, stride=cells), :] = mixed[
                :, y * depth : (y + 1) * depth
            ]
        return 0

    lax.fori_loop(0, size_x, rotate, 0)
    for items in (first, second, third, fourth):
        wait_send(items)


def per_device(
    x_block, old_direction, conductivity, fsai_diagonal, fsai_lower, pattern, step_size, momentum
):
    vectors, size_x, size_y, size_z = x_block.shape
    nx, ny = lax.axis_size("gx"), lax.axis_size("gy")
    cells = size_x * size_y
    scale = 1.0 / (cells * size_z * nx * ny)
    flat = (vectors * cells, size_z)
    column = (vectors, size_z)
    vmem = pl.BlockSpec(memory_space=pltpu.VMEM)
    smem = pl.BlockSpec(memory_space=pltpu.SMEM)

    def padded(rx, ry):
        return pltpu.VMEM((size_x + 2 * rx, size_y + 2 * ry) + column, F32)

    terms = fsai_lower.shape[0] + 1
    x_next, direction, rayleigh = pl.pallas_call(
        functools.partial(kernel, nx, ny, scale),
        out_shape=[
            jax.ShapeDtypeStruct(flat, F32),
            jax.ShapeDtypeStruct(flat, F32),
            jax.ShapeDtypeStruct((vectors, vectors), F32),
        ],
        in_specs=[vmem] * 5 + [smem] * 3,
        out_specs=[vmem] * 3,
        scratch_shapes=[
            padded(1, 1), padded(1, 1), padded(1, 1), padded(1, 2), padded(1, 1), padded(1, 1),
            pltpu.VMEM((size_y,) + column, F32),
            pltpu.VMEM((size_x,) + column, F32),
            pltpu.VMEM((size_x,) + column, F32),
            pltpu.VMEM((2,) + column, F32),
            pltpu.VMEM((size_y,) + column, F32),
            pltpu.VMEM((size_x,) + column, F32),
            pltpu.VMEM((4, size_y, size_z), F32),
            pltpu.VMEM((2, size_x, size_z), F32),
            pltpu.VMEM((7, size_x, size_y, size_z), F32),
            pltpu.VMEM((terms, size_x + 2, size_y + 8, size_z), F32),
            pltpu.VMEM((terms - 1, size_x, size_y, size_z), F32),
            pltpu.VMEM((6 * vectors, cells * size_z), BF16),
            pltpu.VMEM((6 * vectors, (size_x + size_y) * size_z), BF16),
            pltpu.VMEM((nx,) + column, F32),
            pltpu.VMEM((ny,) + column, F32),
            pltpu.VMEM((nx,) + column, F32),
            pltpu.VMEM((ny,) + column, F32),
            pltpu.SemaphoreType.DMA((22,)),
            pltpu.SemaphoreType.DMA((22,)),
            pltpu.SemaphoreType.DMA((2, nx)),
            pltpu.SemaphoreType.DMA((2, nx)),
            pltpu.SemaphoreType.DMA((2, ny)),
            pltpu.SemaphoreType.DMA((2, ny)),
        ],
        compiler_params=pltpu.CompilerParams(
            collective_id=0, has_side_effects=True, vmem_limit_bytes=48 * 1024 * 1024
        ),
    )(
        x_block.reshape(flat), old_direction.reshape(flat), conductivity, fsai_diagonal,
        fsai_lower, pattern, step_size, momentum,
    )
    return x_next.reshape(x_block.shape), direction.reshape(x_block.shape), rayleigh


def solution(mesh):
    placed = (
        P(None, "gx", "gy", None),
        P(None, "gx", "gy", None),
        P("gx", "gy", None),
        P("gx", "gy", None),
        P(None, "gx", "gy", None),
        P(),
        P(),
        P(),
    )
    return jax.shard_map(
        per_device,
        mesh=mesh,
        in_specs=placed,
        out_specs=(P(None, "gx", "gy", None), P(None, "gx", "gy", None), P()),
        check_vma=False,
    )
```

time: 180 us -> 51.1 us (0.28)
  blocking collectives: 88.1 us -> 0 us
  starting transfers between devices: 46.1 us -> 0 us
  Pallas kernels: 0 us -> 41.9 us
  waiting for transfers between devices: 16.5 us -> 0 us
  other arithmetic: 14 us -> 0 us
  matrix products: 5.21 us -> 0 us
    psum x2 -> x0, blocking collectives: 88.1 us -> none  [the longest x1 44.4 us: quotient_of(): sum_xx, sum_xa = lax.psum((local_xx, local_xa), ('gx', 'gy'))]
    ppermute x19 -> x0, starting transfers between devices: 46.1 us -> none  [the longest x9 33.2 us: extended(): lax.ppermute(tail, axis, [(i, (i + 1) % count) for i in range(ends)])]
    pallas_call x0 -> x1, Pallas kernels: none -> 41.9 us  [per_device(): pl.pallas_call(functools.partial(kernel, nx, ny, scale), out_shape=[jax.S...]
    ppermute x19 -> x0, waiting for transfers between devices: 16.5 us -> none  [the longest x9 13.2 us: extended(): lax.ppermute(head, axis, [((i + 1) % count, i) for i in range(ends)])]
    dot_general x6 -> x0, matrix products: 5.02 us -> none  [the longest x1 1.36 us: per_device(): jnp.einsum('kxyz,jxyz->kj', advanced, advanced_image, precision=lax.Preci...]
    unnamed x41 -> x19, local copies, waits for them, and re-layouts: 3.19 us -> 8.13 us
    concatenate x9 -> x0, other arithmetic: 4.52 us -> none  [the longest x7 4.35 us: extended(): jnp.concatenate([lax.ppermute(tail, axis, [(i, (i + 1) % count) for i in...]
    another operation x5 -> x0, other arithmetic: 4.01 us -> none  [the longest x3 2.13 us: per_device(): factor = jnp.linalg.cholesky(gram)]
  transfers between devices with their start and end apart: 19 -> 0, of which waited for: 6 -> 0; matrix products, arithmetic and copies ran while one was open for 5% -> 0% of each run, Pallas kernels for 0% -> 0%
where the time goes in v1:
time: 51.1 us; the launch traced here: 50.7 us
  Pallas kernels  41.9 us (82%)
  local copies, waits for them, and re-layouts  8.13 us (16%)
  between operations  0.67 us (1%)
    pallas_call x1, Pallas kernels, per_device(): pl.pallas_call(functools.partial(kernel, nx, ny, scale), out_shape=[jax.S...  41.9 us
    unnamed x19, local copies, waits for them, and re-layouts  8.13 us

profile of v1, /device:TPU:0, one launch (start us, length us, event | category | flops | bytes accessed | tf_op | source)
XLA Modules:
  0.0 50.7 jit_solution(17105414208547694518)
XLA Ops:
  0.6 0.0 copy-start.6
  0.6 0.0 copy-start.7
  0.7 0.6 %copy-done.6 = f32[16]{0:T(128)S(1)} copy-done((f32[16]{0:T(128)S(1)}, f32[16]{0:T(128)}, u32[]{:S(2)}) %copy-start.6) | copy-done | bytes 88
  1.3 0.0 copy-done.7
  1.3 0.0 copy-start
  1.3 1.0 %copy-done = f32[16,8,8,128]{3,2,1,0:T(8,128)S(1)} copy-done((f32[16,8,8,128]{3,2,1,0:T(8,128)S(1)}, f32[16,8,8,128]{3,2,1,0:T(8,128)}, u32[]{:S(2)}) %copy-start) | copy-done | bytes 524312
  2.3 0.0 copy-start.1
  2.3 1.0 %copy-done.1 = f32[16,8,8,128]{3,2,1,0:T(8,128)S(1)} copy-done((f32[16,8,8,128]{3,2,1,0:T(8,128)S(1)}, f32[16,8,8,128]{3,2,1,0:T(8,128)}, u32[]{:S(2)}) %copy-start.1) | copy-done | bytes 524312
  3.4 0.0 copy-start.2
  3.4 1.0 %copy-done.2 = f32[13,8,8,128]{3,2,1,0:T(8,128)S(1)} copy-done((f32[13,8,8,128]{3,2,1,0:T(8,128)S(1)}, f32[13,8,8,128]{3,2,1,0:T(8,128)}, u32[]{:S(2)}) %copy-start.2) | copy-done | bytes 426008
  4.4 0.0 copy-start.3
  4.4 0.8 %copy-done.3 = f32[8,8,128]{2,1,0:T(8,128)S(1)} copy-done((f32[8,8,128]{2,1,0:T(8,128)S(1)}, f32[8,8,128]{2,1,0:T(8,128)}, u32[]{:S(2)}) %copy-start.3) | copy-done | bytes 32792
  5.2 0.0 copy-start.4
  5.2 0.8 %copy-done.4 = f32[8,8,128]{2,1,0:T(8,128)S(1)} copy-done((f32[8,8,128]{2,1,0:T(8,128)S(1)}, f32[8,8,128]{2,1,0:T(8,128)}, u32[]{:S(2)}) %copy-start.4) | copy-done | bytes 32792
  5.9 0.0 copy-start.5
  5.9 0.7 %copy-done.5 = s32[8,13]{1,0:T(8,128)S(1)} copy-done((s32[8,13]{1,0:T(8,128)S(1)}, s32[8,13]{1,0:T(8,128)}, u32[]{:S(2)}) %copy-start.5) | copy-done | bytes 440
  6.6 41.9 %shard_map.103 = (f32[1024,128]{1,0:T(8,128)S(1)}, f32[1024,128]{1,0:T(8,128)S(1)}, f32[16,16]{1,0:T(8,128)S(1)}) custom-call(f32[1024,128]{1,0:T(8,128)S(1)} %bitcast.6, f32[1024,128]{1,0:T(8,128)S(1)} %bitcast.7, f32[8,8,128]{2,1,0:T(8,128)S(1)} %copy-done.3, f32[8,8,128]{2,1,0:T(8,128)S(1)} %copy-done.4, f32[13,8,8,128]{3,2,1,0:T(8,128)S(1)} %copy-done.2, ...), custom_call_target="tpu_custom_call" | custom-call | tf_op jit(solution)/shard_map/pallas_call | solution.py:474
  48.5 0.8 %copy.14 = f32[16,8,8,128]{3,2,1,0:T(8,128)} copy(f32[16,8,8,128]{3,2,1,0:T(8,128)S(1)} %bitcast.5) | data formatting | bytes 1048576
  49.3 0.8 %copy.15 = f32[16,8,8,128]{3,2,1,0:T(8,128)} copy(f32[16,8,8,128]{3,2,1,0:T(8,128)S(1)} %bitcast.4) | data formatting | bytes 1048576
  50.1 0.6 %copy.16 = f32[16,16]{1,0:T(8,128)} copy(f32[16,16]{1,0:T(8,128)S(1)} %get-tuple-element.14) | data formatting | bytes 2048
Async XLA Ops:
  0.6 0.7 %copy-start.6 = (f32[16]{0:T(128)S(1)}, f32[16]{0:T(128)}, u32[]{:S(2)}) copy-start(f32[16]{0:T(128)} %step_in.1) | copy-start | bytes 196
  0.6 0.7 %copy-start.7 = (f32[16]{0:T(128)S(1)}, f32[16]{0:T(128)}, u32[]{:S(2)}) copy-start(f32[16]{0:T(128)} %mom_in.1) | copy-start | bytes 196
  1.3 1.0 %copy-start = (f32[16,8,8,128]{3,2,1,0:T(8,128)S(1)}, f32[16,8,8,128]{3,2,1,0:T(8,128)}, u32[]{:S(2)}) copy-start(f32[16,8,8,128]{3,2,1,0:T(8,128)} %param.8) | copy-start | bytes 1572868
  2.3 1.0 %copy-start.1 = (f32[16,8,8,128]{3,2,1,0:T(8,128)S(1)}, f32[16,8,8,128]{3,2,1,0:T(8,128)}, u32[]{:S(2)}) copy-start(f32[16,8,8,128]{3,2,1,0:T(8,128)} %param.9) | copy-start | bytes 1572868
  3.4 1.0 %copy-start.2 = (f32[13,8,8,128]{3,2,1,0:T(8,128)S(1)}, f32[13,8,8,128]{3,2,1,0:T(8,128)}, u32[]{:S(2)}) copy-start(f32[13,8,8,128]{3,2,1,0:T(8,128)} %lower_in.1) | copy-start | bytes 1277956
  4.4 0.8 %copy-start.3 = (f32[8,8,128]{2,1,0:T(8,128)S(1)}, f32[8,8,128]{2,1,0:T(8,128)}, u32[]{:S(2)}) copy-start(f32[8,8,128]{2,1,0:T(8,128)} %cond_in.1) | copy-start | bytes 98308
  5.2 0.8 %copy-start.4 = (f32[8,8,128]{2,1,0:T(8,128)S(1)}, f32[8,8,128]{2,1,0:T(8,128)}, u32[]{:S(2)}) copy-start(f32[8,8,128]{2,1,0:T(8,128)} %diag_in.1) | copy-start | bytes 98308
  5.9 0.7 %copy-start.5 = (s32[8,13]{1,0:T(8,128)S(1)}, s32[8,13]{1,0:T(8,128)}, u32[]{:S(2)}) copy-start(s32[8,13]{1,0:T(8,128)} %pattern_in.1) | copy-start | bytes 1252

commit v2 on v1

--- a/solution.py
+++ b/solution.py
@@ -28,14 +28,24 @@
 
 def kernel(
     nx, ny, scale,
+    x_hbm, old_hbm, cond_hbm, diag_hbm, lower_hbm, pattern_hbm, step_hbm, mom_hbm,
+    next_out, dir_out, ray_out,
     x_in, old_in, cond_in, diag_in, lower_in, pattern_in, step_in, mom_in,
-    next_out, dir_out, ray_out,
-    xs, im, gr, pr, pt, adv,
-    recv_x, recv_y0, recv_y1, recv_c, halo_x, halo_y,
+    xs, im, pr, ptx, pt, adv,
+    rx_x, rx_y0, rx_y1, rx_c, recv_x, recv_y0, recv_y1, recv_c, halo_x, halo_y,
     k_side, k_stage, coef, lm, lp,
-    ab, abh, q_x, q_y, g_x, g_y,
-    send_sem, recv_sem, send_x, recv_gx, send_y, recv_gy,
+    ab, abh, q_x, q_y, g_x, g_y, s_x, s_y,
+    load_sem, send_sem, recv_sem, send_x, recv_gx, send_y, recv_gy,
 ):
+    loads = [
+        pltpu.make_async_copy(src, dst, load_sem.at[i])
+        for i, (src, dst) in enumerate((
+            (x_hbm, x_in), (cond_hbm, cond_in), (pattern_hbm, pattern_in), (lower_hbm, lower_in),
+            (diag_hbm, diag_in), (step_hbm, step_in), (mom_hbm, mom_in), (old_hbm, old_in),
+        ))
+    ]
+    for load in loads:
+        load.start()
     ix, iy = lax.axis_index("gx"), lax.axis_index("gy")
     size_x, size_y = cond_in.shape[0], cond_in.shape[1]
     depth = cond_in.shape[2]
@@ -105,13 +115,15 @@
         buf_x[ix] = tile
         group_start(buf_x, turn, nx, ix, along_x, send_x, recv_gx)
 
-    def reduce_finish(buf_x, buf_y, turn):
+    def reduce_middle(buf_x, buf_y, turn):
         group_wait(buf_x, turn, nx, ix, along_x, send_x, recv_gx)
         total = buf_x[0]
         for i in range(1, nx):
             total = total + buf_x[i]
         buf_y[iy] = total
         group_start(buf_y, turn, ny, iy, along_y, send_y, recv_gy)
+
+    def reduce_finish(buf_y, turn):
         group_wait(buf_y, turn, ny, iy, along_y, send_y, recv_gy)
         total = buf_y[0]
         for i in range(1, ny):
@@ -127,15 +139,9 @@
             buf[x, size_y + 1] = zero_col
     for i in range(4):
         k_side[i] = zero_tile
-    for i in range(size_y):
-        recv_x[i] = zero_col
-        halo_x[i] = zero_col
-    for i in range(size_x):
-        recv_y0[i] = zero_col
-        recv_y1[i] = zero_col
-        halo_y[i] = zero_col
-    recv_c[0] = zero_col
-    recv_c[1] = zero_col
+    for buf in (rx_x, rx_y0, rx_y1, rx_c, recv_x, recv_y0, recv_y1, recv_c, halo_x, halo_y):
+        for i in range(buf.shape[0]):
+            buf[i] = zero_col
 
     barrier = pltpu.get_barrier_semaphore()
     for s in range(1, nx):
@@ -151,6 +157,9 @@
             @pl.when(there)
             def _(sx=sx, sy=sy):
                 pl.semaphore_signal(barrier, inc=1, device_id=(ix + sx, iy + sy), device_id_type=MESH)
+
+    loads[0].wait()
+    loads[1].wait()
 
     def turn_in(x, _):
         for y in range(size_y):
@@ -178,6 +187,8 @@
     ]
     start(first)
 
+    for load in loads[2:]:
+        load.wait()
     lane = lax.broadcasted_iota(jnp.int32, (size_y, depth), 1)
     piece = lane // (depth // blocks)
     for o in range(DIAG):
@@ -188,19 +199,13 @@
         if dz:
             keep = jnp.where(lane == (0 if dz < 0 else depth - 1), 0.0, keep)
 
-        def fill(x, _, o=o, dz=dz, keep=keep):
+        for x in range(size_x):
             term = lower_in[o, x] * keep
             lm[o, x + 1, pl.ds(2, size_y), :] = term
             lp[o, x] = pltpu.roll(term, dz % depth, 1) if dz else term
-            return 0
-
-        lax.fori_loop(0, size_x, fill, 0)
-
-    def fill_diag(x, _):
+
+    for x in range(size_x):
         lm[DIAG, x + 1, pl.ds(2, size_y), :] = diag_in[x]
-        return 0
-
-    lax.fori_loop(0, size_x, fill_diag, 0)
 
     def rims(o, _):
         for x in range(size_x + 2):
@@ -234,10 +239,10 @@
     wait_recv(first[:4])
     row8 = lax.broadcasted_iota(jnp.int32, (size_y, depth), 0)
 
-    def faces(x, _):
+    for x in range(size_x):
         here = cond_in[x]
-        below = jnp.where(x == 0, k_side[0], cond_in[jnp.maximum(x - 1, 0)])
-        above = jnp.where(x == size_x - 1, k_side[1], cond_in[jnp.minimum(x + 1, size_x - 1)])
+        below = k_side[0] if x == 0 else cond_in[x - 1]
+        above = k_side[1] if x == size_x - 1 else cond_in[x + 1]
         left = jnp.where(row8 == 0, k_side[2, pl.ds(x, 1), :], pltpu.roll(here, 1, 0))
         right = jnp.where(row8 == size_y - 1, k_side[3, pl.ds(x, 1), :], pltpu.roll(here, size_y - 1, 0))
         back = jnp.where(lane == 0, 0.0, pltpu.roll(here, 1, 1))
@@ -252,9 +257,6 @@
                 face = jnp.where(lane == depth - 1, 0.0, face)
             coef[i + 1, x] = face
         coef[0, x] = total
-        return 0
-
-    lax.fori_loop(0, size_x, faces, 0)
 
     def stiffness(buf, x, y):
         centre = buf[x + 1, y + 1]
@@ -287,7 +289,6 @@
         lane16 < depth // 2,
         jnp.sum(sum_xx, axis=1, keepdims=True), jnp.sum(sum_xa, axis=1, keepdims=True),
     )
-    reduce_start(q_x, 0, both)
     second = [
         (im.at[inner_x, size_y], im.at[inner_x, 0], 0, 1, 10),
         (im.at[inner_x, 1], im.at[inner_x, size_y + 1], 0, -1, 11),
@@ -296,68 +297,79 @@
         (im.at[size_x, 1], im.at[0, size_y + 1], 1, -1, 14),
     ]
     start(second)
-    both = reduce_finish(q_x, q_y, 0)
+    reduce_start(q_x, 0, both)
+
+    def factor(buf):
+        def products(x, _):
+            for y in range(size_y):
+                parts = {0: diag_in[x, pl.ds(y, 1), :] * buf[x + 1, y + 1], -1: zero_col, 1: zero_col}
+                for o, (dx, dy, dz) in enumerate(lower_offsets):
+                    parts[dz] = parts[dz] + lp[o, x, pl.ds(y, 1), :] * buf[x + 1 + dx, y + 1 + dy]
+                pr[x + 1, y + 2] = (
+                    parts[0] + pltpu.roll(parts[-1], 1, 1) + pltpu.roll(parts[1], depth - 1, 1)
+                )
+            return 0
+
+        lax.fori_loop(0, size_x, products, 0)
+
+    def transposed(out, arrivals, slot):
+        def target(x, y):
+            parts = {0: lm[DIAG, x, pl.ds(y + 1, 1), :] * pr[x, y + 1], -1: zero_col, 1: zero_col}
+            for o, (dx, dy, dz) in enumerate(lower_offsets):
+                parts[dz] = parts[dz] + lm[o, x - dx, pl.ds(y + 1 - dy, 1), :] * pr[x - dx, y + 1 - dy]
+            out[x, y] = parts[0] + pltpu.roll(parts[-1], depth - 1, 1) + pltpu.roll(parts[1], 1, 1)
+
+        for y in range(size_y + 2):
+            target(0, y)
+
+        def rim_targets(x, _):
+            target(x, 0)
+            target(x, size_y + 1)
+            return 0
+
+        lax.fori_loop(1, size_x + 1, rim_targets, 0)
+        to_x, to_y0, to_y1, to_c = arrivals
+        items = [
+            (out.at[inner_x, 0], to_y0, 0, -1, slot),
+            (out.at[inner_x, size_y + 1], to_y1, 0, 1, slot + 1),
+            (out.at[0, inner_y], to_x, -1, 0, slot + 2),
+            (out.at[0, 0], to_c.at[0], -1, -1, slot + 3),
+            (out.at[0, size_y + 1], to_c.at[1], -1, 1, slot + 4),
+        ]
+        start(items)
+
+        def own_targets(x, _):
+            for y in range(1, size_y + 1):
+                target(x, y)
+            return 0
+
+        lax.fori_loop(1, size_x + 1, own_targets, 0)
+        return items
+
+    def gather(out, arrivals, items):
+        wait_recv(items)
+        to_x, to_y0, to_y1, to_c = arrivals
+        for y in range(size_y):
+            out[size_x, y + 1] = out[size_x, y + 1] + to_x[y]
+        for x in range(size_x):
+            out[x + 1, size_y] = out[x + 1, size_y] + to_y0[x]
+            out[x + 1, 1] = out[x + 1, 1] + to_y1[x]
+        out[size_x, size_y] = out[size_x, size_y] + to_c[0]
+        out[size_x, 1] = out[size_x, 1] + to_c[1]
+
+    arrivals_x = (rx_x, rx_y0, rx_y1, rx_c)
+    arrivals = (recv_x, recv_y0, recv_y1, recv_c)
+    factor(xs)
+    third_x = transposed(ptx, arrivals_x, 22)
+    reduce_middle(q_x, q_y, 0)
+    wait_recv(second)
+    factor(im)
+    third = transposed(pt, arrivals, 15)
+    gather(ptx, arrivals_x, third_x)
+    both = reduce_finish(q_y, 0)
     quotient = both[:, depth // 2 : depth // 2 + 1] * scale / (both[:, 0:1] * scale + 1e-06)
     quotient = jnp.broadcast_to(quotient, (vectors, depth))
-    wait_recv(second)
-
-    def gradients(x, _):
-        for y in range(size_y + 2):
-            gr[x, y] = im[x, y] - quotient * xs[x, y]
-        return 0
-
-    lax.fori_loop(0, size_x + 1, gradients, 0)
-
-    def products(x, _):
-        for y in range(size_y):
-            parts = {0: diag_in[x, pl.ds(y, 1), :] * gr[x + 1, y + 1], -1: zero_col, 1: zero_col}
-            for o, (dx, dy, dz) in enumerate(lower_offsets):
-                parts[dz] = parts[dz] + lp[o, x, pl.ds(y, 1), :] * gr[x + 1 + dx, y + 1 + dy]
-            pr[x + 1, y + 2] = (
-                parts[0] + pltpu.roll(parts[-1], 1, 1) + pltpu.roll(parts[1], depth - 1, 1)
-            )
-        return 0
-
-    lax.fori_loop(0, size_x, products, 0)
-
-    def target(x, y):
-        parts = {0: lm[DIAG, x, pl.ds(y + 1, 1), :] * pr[x, y + 1], -1: zero_col, 1: zero_col}
-        for o, (dx, dy, dz) in enumerate(lower_offsets):
-            parts[dz] = parts[dz] + lm[o, x - dx, pl.ds(y + 1 - dy, 1), :] * pr[x - dx, y + 1 - dy]
-        pt[x, y] = parts[0] + pltpu.roll(parts[-1], depth - 1, 1) + pltpu.roll(parts[1], 1, 1)
-
-    for y in range(size_y + 2):
-        target(0, y)
-
-    def rim_targets(x, _):
-        target(x, 0)
-        target(x, size_y + 1)
-        return 0
-
-    lax.fori_loop(1, size_x + 1, rim_targets, 0)
-    third = [
-        (pt.at[inner_x, 0], recv_y0, 0, -1, 15),
-        (pt.at[inner_x, size_y + 1], recv_y1, 0, 1, 16),
-        (pt.at[0, inner_y], recv_x, -1, 0, 17),
-        (pt.at[0, 0], recv_c.at[0], -1, -1, 18),
-        (pt.at[0, size_y + 1], recv_c.at[1], -1, 1, 19),
-    ]
-    start(third)
-
-    def own_targets(x, _):
-        for y in range(1, size_y + 1):
-            target(x, y)
-        return 0
-
-    lax.fori_loop(1, size_x + 1, own_targets, 0)
-    wait_recv(third)
-    for y in range(size_y):
-        pt[size_x, y + 1] = pt[size_x, y + 1] + recv_x[y]
-    for x in range(size_x):
-        pt[x + 1, size_y] = pt[x + 1, size_y] + recv_y0[x]
-        pt[x + 1, 1] = pt[x + 1, 1] + recv_y1[x]
-    pt[size_x, size_y] = pt[size_x, size_y] + recv_c[0]
-    pt[size_x, 1] = pt[size_x, 1] + recv_c[1]
+    gather(pt, arrivals, third)
 
     def at_column(index):
         return pl.ds(pl.multiple_of(index * depth, depth), depth)
@@ -369,7 +381,7 @@
     def advance(x, _):
         for y in range(size_y):
             spot = pl.ds(x * size_y + y, vectors, stride=cells)
-            direction = pt[x + 1, y + 1] + mom_col * old_in[spot, :]
+            direction = (pt[x + 1, y + 1] - quotient * ptx[x + 1, y + 1]) + mom_col * old_in[spot, :]
             dir_out[spot, :] = direction
             advanced = xs[x + 1, y + 1] + step_col * direction
             adv[x + 1, y + 1] = advanced
@@ -382,67 +394,64 @@
         (adv.at[1, inner_y], halo_x, -1, 0, 21),
     ]
     start(fourth)
+    nt = (((1,), (1,)), ((), ()))
+    third_rows = 3 * vectors
+
+    def collect(array):
+        return sum(
+            array[i * vectors : (i + 1) * vectors, j * vectors : (j + 1) * vectors]
+            for i in range(3) for j in range(3)
+        )
+
+    def as_tile(array):
+        return jnp.concatenate([array, jnp.zeros((vectors, depth - vectors), F32)], axis=1)
+
+    gram = collect(lax.dot_general(
+        ab[0:third_rows, :], ab[0:third_rows, :], nt, preferred_element_type=F32
+    ))
+    reduce_start(g_x, 1, as_tile(gram))
 
     def advanced_images(x, _):
         for y in range(size_y):
-            put(ab, 3 * vectors, x * size_y + y, stiffness(adv, x, y))
+            put(ab, third_rows, x * size_y + y, stiffness(adv, x, y))
         return 0
 
     lax.fori_loop(0, size_x, advanced_images, 0)
-    nt = (((1,), (1,)), ((), ()))
-    grams = lax.dot_general(ab[0 : 3 * vectors, :], ab[...], nt, preferred_element_type=F32)
+    reduce_middle(g_x, g_y, 1)
+    stiff = collect(lax.dot_general(
+        ab[0:third_rows, :], ab[third_rows:, :], nt, preferred_element_type=F32
+    ))
     wait_recv(fourth)
     for y in range(size_y):
         put(abh, 0, y, adv[size_x, y + 1])
-        put(abh, 3 * vectors, y, -coef[2, size_x - 1, pl.ds(y, 1), :] * halo_x[y])
+        put(abh, third_rows, y, -coef[2, size_x - 1, pl.ds(y, 1), :] * halo_x[y])
     for x in range(size_x):
         put(abh, 0, size_y + x, adv[x + 1, size_y])
-        put(abh, 3 * vectors, size_y + x, -coef[4, x, pl.ds(size_y - 1, 1), :] * halo_y[x])
+        put(abh, third_rows, size_y + x, -coef[4, x, pl.ds(size_y - 1, 1), :] * halo_y[x])
     crossed = lax.dot_general(abh[...], abh[...], nt, preferred_element_type=F32)
-
-    def rows(array, base):
-        return (
-            array[base : base + vectors]
-            + array[base + vectors : base + 2 * vectors]
-            + array[base + 2 * vectors : base + 3 * vectors]
-        )
-
-    def wide(array):
-        return jnp.concatenate([array, jnp.zeros((vectors, depth - 6 * vectors), F32)], axis=1)
-
-    def lanes(array):
-        return (
-            array + pltpu.roll(array, depth - vectors, 1) + pltpu.roll(array, depth - 2 * vectors, 1)
-        )
-
-    main = lanes(wide(rows(grams, 0)))
-    upper = lanes(wide(rows(crossed, 0)))
-    lower = lanes(wide(rows(crossed, 3 * vectors)))
-    stiff = pltpu.roll(main + upper, depth - 2 * vectors, 1) + pltpu.roll(lower, vectors, 1)
-    packed = jnp.where(lane16 < vectors, main, jnp.where(lane16 < 2 * vectors, stiff, 0.0))
-    reduce_start(g_x, 1, packed)
-    packed = reduce_finish(g_x, g_y, 1) * scale
-
-    aug = packed + jnp.where(row == lane16, 1e-05, 0.0)
-    aug = aug + jnp.where(row + 2 * vectors == lane16, 1.0, 0.0)
+    stiff = stiff + collect(crossed[0:third_rows, third_rows:]) + collect(crossed[third_rows:, 0:third_rows])
+    reduce_start(s_x, 2, as_tile(stiff))
+
+    aug = reduce_finish(g_y, 1) * scale + jnp.where(row == lane16, 1e-05, 0.0)
+    aug = aug + jnp.where(row + vectors == lane16, 1.0, 0.0)
     for j in range(vectors - 1):
         ratio = aug[:, j : j + 1] / aug[j : j + 1, j : j + 1]
         aug = aug - jnp.where(row > j, ratio * aug[j : j + 1, :], 0.0)
     pivots = jnp.sum(jnp.where(row == lane16, aug, 0.0), axis=1, keepdims=True)
     aug = aug / jnp.sqrt(pivots)
-    inverse = aug[:, 2 * vectors : 3 * vectors]
-    ray_out[...] = lax.dot_general(
-        aug[:, vectors : 2 * vectors], inverse, nt,
-        preferred_element_type=F32, precision=lax.Precision.HIGHEST,
-    )
+    inverse = aug[:, vectors : 2 * vectors]
+    reduce_middle(s_x, s_y, 2)
     weights = jnp.concatenate(
         [jnp.concatenate([part.astype(F32)] * 3, axis=1) for part in split3(inverse)], axis=0
     ).astype(BF16)
 
+    def rows(array):
+        return array[:vectors] + array[vectors : 2 * vectors] + array[2 * vectors :]
+
     def rotate(x, _):
         wide_part = pl.ds(pl.multiple_of(x * size_y * depth, depth), size_y * depth)
         mixed = rows(
-            jnp.dot(weights, ab[0 : 3 * vectors, wide_part], preferred_element_type=F32), 0
+            jnp.dot(weights, ab[0 : 3 * vectors, wide_part], preferred_element_type=F32)
         )
         for y in range(size_y):
             next_out[pl.ds(x * size_y + y, vectors, stride=cells), :] = mixed[
@@ -451,7 +460,11 @@
         return 0
 
     lax.fori_loop(0, size_x, rotate, 0)
-    for items in (first, second, third, fourth):
+    stiff = (reduce_finish(s_y, 2) * scale)[:, 0:vectors]
+    highest = lax.Precision.HIGHEST
+    half = jnp.dot(inverse, stiff, preferred_element_type=F32, precision=highest)
+    ray_out[...] = lax.dot_general(half, inverse, nt, preferred_element_type=F32, precision=highest)
+    for items in (first, second, third_x, third, fourth):
         wait_send(items)
 
 
@@ -465,7 +478,7 @@
     flat = (vectors * cells, size_z)
     column = (vectors, size_z)
     vmem = pl.BlockSpec(memory_space=pltpu.VMEM)
-    smem = pl.BlockSpec(memory_space=pltpu.SMEM)
+    hbm = pl.BlockSpec(memory_space=pltpu.HBM)
 
     def padded(rx, ry):
         return pltpu.VMEM((size_x + 2 * rx, size_y + 2 * ry) + column, F32)
@@ -478,10 +491,22 @@
             jax.ShapeDtypeStruct(flat, F32),
             jax.ShapeDtypeStruct((vectors, vectors), F32),
         ],
-        in_specs=[vmem] * 5 + [smem] * 3,
+        in_specs=[hbm] * 8,
         out_specs=[vmem] * 3,
         scratch_shapes=[
-            padded(1, 1), padded(1, 1), padded(1, 1), padded(1, 2), padded(1, 1), padded(1, 1),
+            pltpu.VMEM(flat, F32),
+            pltpu.VMEM(flat, F32),
+            pltpu.VMEM(conductivity.shape, F32),
+            pltpu.VMEM(fsai_diagonal.shape, F32),
+            pltpu.VMEM(fsai_lower.shape, F32),
+            pltpu.SMEM(pattern.shape, jnp.int32),
+            pltpu.SMEM(step_size.shape, F32),
+            pltpu.SMEM(momentum.shape, F32),
+            padded(1, 1), padded(1, 1), padded(1, 2), padded(1, 1), padded(1, 1), padded(1, 1),
+            pltpu.VMEM((size_y,) + column, F32),
+            pltpu.VMEM((size_x,) + column, F32),
+            pltpu.VMEM((size_x,) + column, F32),
+            pltpu.VMEM((2,) + column, F32),
             pltpu.VMEM((size_y,) + column, F32),
             pltpu.VMEM((size_x,) + column, F32),
             pltpu.VMEM((size_x,) + column, F32),
@@ -499,15 +524,18 @@
             pltpu.VMEM((ny,) + column, F32),
             pltpu.VMEM((nx,) + column, F32),
             pltpu.VMEM((ny,) + column, F32),
-            pltpu.SemaphoreType.DMA((22,)),
-            pltpu.SemaphoreType.DMA((22,)),
-            pltpu.SemaphoreType.DMA((2, nx)),
-            pltpu.SemaphoreType.DMA((2, nx)),
-            pltpu.SemaphoreType.DMA((2, ny)),
-            pltpu.SemaphoreType.DMA((2, ny)),
+            pltpu.VMEM((nx,) + column, F32),
+            pltpu.VMEM((ny,) + column, F32),
+            pltpu.SemaphoreType.DMA((8,)),
+            pltpu.SemaphoreType.DMA((27,)),
+            pltpu.SemaphoreType.DMA((27,)),
+            pltpu.SemaphoreType.DMA((3, nx)),
+            pltpu.SemaphoreType.DMA((3, nx)),
+            pltpu.SemaphoreType.DMA((3, ny)),
+            pltpu.SemaphoreType.DMA((3, ny)),
         ],
         compiler_params=pltpu.CompilerParams(
-            collective_id=0, has_side_effects=True, vmem_limit_bytes=48 * 1024 * 1024
+            collective_id=0, has_side_effects=True, vmem_limit_bytes=62 * 1024 * 1024
         ),
     )(
         x_block.reshape(flat), old_direction.reshape(flat), conductivity, fsai_diagonal,

time: 51.1 us -> 45.5 us (0.89)
  local copies, waits for them, and re-layouts: 8.13 us -> 3.34 us
    unnamed x19 -> x7, local copies, waits for them, and re-layouts: 8.13 us -> 3.34 us
where the time goes in v2:
time: 45.5 us; the launch traced here: 45.4 us
  Pallas kernels  41.4 us (91%)
  local copies, waits for them, and re-layouts  3.34 us (7%)
  between operations  0.65 us (1%)
    pallas_call x1, Pallas kernels, per_device(): pl.pallas_call(functools.partial(kernel, nx, ny, scale), out_shape=[jax.S...  41.4 us
    unnamed x7, local copies, waits for them, and re-layouts  3.34 us

profile of v2, /device:TPU:0, one launch (start us, length us, event | category | flops | bytes accessed | tf_op | source)
XLA Modules:
  0.0 45.4 jit_solution(6266435278706556406)
XLA Ops:
  0.6 41.4 %shard_map.103 = (f32[1024,128]{1,0:T(8,128)}, f32[1024,128]{1,0:T(8,128)}, f32[16,16]{1,0:T(8,128)}) custom-call(f32[1024,128]{1,0:T(8,128)} %bitcast.6, f32[1024,128]{1,0:T(8,128)} %bitcast.7, f32[8,8,128]{2,1,0:T(8,128)} %cond_hbm.1, f32[8,8,128]{2,1,0:T(8,128)} %diag_hbm.1, f32[13,8,8,128]{3,2,1,0:T(8,128)} %lower_hbm.1, s32[8,13]{1,0:T(8,128)} %pattern_hbm.1, ...), custom_call_target="tpu_custom_call" | custom-call | tf_op jit(solution)/shard_map/pallas_call | solution.py:487
  42.0 0.0 copy-start
  42.0 1.9 %copy.14 = f32[16,8,8,128]{3,2,1,0:T(8,128)} copy(f32[16,8,8,128]{3,2,1,0:T(8,128)} %bitcast.5) | data formatting | bytes 1048576
  44.0 0.0 copy-done
  44.0 0.0 copy-start.1
  44.0 0.8 %copy.15 = f32[16,8,8,128]{3,2,1,0:T(8,128)} copy(f32[16,8,8,128]{3,2,1,0:T(8,128)S(1)} %bitcast.4) | data formatting | bytes 1048576
  44.8 0.0 copy-done.1
  44.8 0.6 %copy.16 = f32[16,16]{1,0:T(8,128)} copy(f32[16,16]{1,0:T(8,128)S(1)} %copy-done.1) | data formatting | bytes 2048
Async XLA Ops:
  42.0 2.0 %copy-start = (f32[1024,128]{1,0:T(8,128)S(1)}, f32[1024,128]{1,0:T(8,128)}, u32[]{:S(2)}) copy-start(f32[1024,128]{1,0:T(8,128)} %get-tuple-element.7) | copy-start | bytes 1572868
  44.0 0.8 %copy-start.1 = (f32[16,16]{1,0:T(8,128)S(1)}, f32[16,16]{1,0:T(8,128)}, u32[]{:S(2)}) copy-start(f32[16,16]{1,0:T(8,128)} %get-tuple-element.14) | copy-start | bytes 3076

commit v3 on v2

--- a/solution.py
+++ b/solution.py
@@ -29,12 +29,13 @@
 def kernel(
     nx, ny, scale,
     x_hbm, old_hbm, cond_hbm, diag_hbm, lower_hbm, pattern_hbm, step_hbm, mom_hbm,
-    next_out, dir_out, ray_out,
+    next_hbm, dir_hbm, ray_out,
     x_in, old_in, cond_in, diag_in, lower_in, pattern_in, step_in, mom_in,
     xs, im, pr, ptx, pt, adv,
     rx_x, rx_y0, rx_y1, rx_c, recv_x, recv_y0, recv_y1, recv_c, halo_x, halo_y,
     k_side, k_stage, coef, lm, lp,
     ab, abh, q_x, q_y, g_x, g_y, s_x, s_y,
+    next_out, dir_out, store_sem,
     load_sem, send_sem, recv_sem, send_x, recv_gx, send_y, recv_gy,
 ):
     loads = [
@@ -271,24 +272,24 @@
             - c(5) * pltpu.roll(centre, 1, 1) - c(6) * pltpu.roll(centre, depth - 1, 1)
         )
 
+    def image_at(x, y, sums):
+        centre = xs[x + 1, y + 1]
+        image = stiffness(xs, x, y)
+        im[x + 1, y + 1] = image
+        return sums[0] + centre * centre, sums[1] + centre * image
+
+    def inner_images(x, sums):
+        for y in range(1, size_y - 1):
+            sums = image_at(x, y, sums)
+        return sums
+
+    def side_images(x, sums):
+        return image_at(x, size_y - 1, image_at(x, 0, sums))
+
+    sums = lax.fori_loop(1, size_x - 1, inner_images, (zero_col, zero_col))
     wait_recv(first[4:])
-
-    def images(x, sums):
-        sum_xx, sum_xa = sums
-        for y in range(size_y):
-            centre = xs[x + 1, y + 1]
-            image = stiffness(xs, x, y)
-            im[x + 1, y + 1] = image
-            sum_xx = sum_xx + centre * centre
-            sum_xa = sum_xa + centre * image
-        return sum_xx, sum_xa
-
-    sum_xx, sum_xa = lax.fori_loop(0, size_x, images, (zero_col, zero_col))
-    lane16 = lax.broadcasted_iota(jnp.int32, (vectors, depth), 1)
-    both = jnp.where(
-        lane16 < depth // 2,
-        jnp.sum(sum_xx, axis=1, keepdims=True), jnp.sum(sum_xa, axis=1, keepdims=True),
-    )
+    sums = lax.fori_loop(0, size_x, side_images, sums)
+    sums = inner_images(size_x - 1, inner_images(0, sums))
     second = [
         (im.at[inner_x, size_y], im.at[inner_x, 0], 0, 1, 10),
         (im.at[inner_x, 1], im.at[inner_x, size_y + 1], 0, -1, 11),
@@ -297,6 +298,12 @@
         (im.at[size_x, 1], im.at[0, size_y + 1], 1, -1, 14),
     ]
     start(second)
+    sum_xx, sum_xa = sums
+    lane16 = lax.broadcasted_iota(jnp.int32, (vectors, depth), 1)
+    both = jnp.where(
+        lane16 < depth // 2,
+        jnp.sum(sum_xx, axis=1, keepdims=True), jnp.sum(sum_xa, axis=1, keepdims=True),
+    )
     reduce_start(q_x, 0, both)
 
     def factor(buf):
@@ -394,6 +401,8 @@
         (adv.at[1, inner_y], halo_x, -1, 0, 21),
     ]
     start(fourth)
+    dir_store = pltpu.make_async_copy(dir_out, dir_hbm, store_sem.at[0])
+    dir_store.start()
     nt = (((1,), (1,)), ((), ()))
     third_rows = 3 * vectors
 
@@ -403,8 +412,14 @@
             for i in range(3) for j in range(3)
         )
 
+    half_rows = vectors // 2
+
     def as_tile(array):
-        return jnp.concatenate([array, jnp.zeros((vectors, depth - vectors), F32)], axis=1)
+        empty = jnp.zeros((half_rows, depth - 2 * vectors), F32)
+        return jnp.concatenate([array[:half_rows], array[half_rows:], empty], axis=1)
+
+    def from_tile(tile):
+        return jnp.concatenate([tile, pltpu.roll(tile, depth - vectors, 1)], axis=0)
 
     gram = collect(lax.dot_general(
         ab[0:third_rows, :], ab[0:third_rows, :], nt, preferred_element_type=F32
@@ -432,7 +447,8 @@
     stiff = stiff + collect(crossed[0:third_rows, third_rows:]) + collect(crossed[third_rows:, 0:third_rows])
     reduce_start(s_x, 2, as_tile(stiff))
 
-    aug = reduce_finish(g_y, 1) * scale + jnp.where(row == lane16, 1e-05, 0.0)
+    total = jnp.where(lane16 < vectors, from_tile(reduce_finish(g_y, 1)), 0.0)
+    aug = total * scale + jnp.where(row == lane16, 1e-05, 0.0)
     aug = aug + jnp.where(row + vectors == lane16, 1.0, 0.0)
     for j in range(vectors - 1):
         ratio = aug[:, j : j + 1] / aug[j : j + 1, j : j + 1]
@@ -460,12 +476,16 @@
         return 0
 
     lax.fori_loop(0, size_x, rotate, 0)
-    stiff = (reduce_finish(s_y, 2) * scale)[:, 0:vectors]
+    next_store = pltpu.make_async_copy(next_out, next_hbm, store_sem.at[1])
+    next_store.start()
+    stiff = (from_tile(reduce_finish(s_y, 2)) * scale)[:, 0:vectors]
     highest = lax.Precision.HIGHEST
     half = jnp.dot(inverse, stiff, preferred_element_type=F32, precision=highest)
     ray_out[...] = lax.dot_general(half, inverse, nt, preferred_element_type=F32, precision=highest)
     for items in (first, second, third_x, third, fourth):
         wait_send(items)
+    dir_store.wait()
+    next_store.wait()
 
 
 def per_device(
@@ -492,7 +512,7 @@
             jax.ShapeDtypeStruct((vectors, vectors), F32),
         ],
         in_specs=[hbm] * 8,
-        out_specs=[vmem] * 3,
+        out_specs=[hbm, hbm, vmem],
         scratch_shapes=[
             pltpu.VMEM(flat, F32),
             pltpu.VMEM(flat, F32),
@@ -522,10 +542,13 @@
             pltpu.VMEM((6 * vectors, (size_x + size_y) * size_z), BF16),
             pltpu.VMEM((nx,) + column, F32),
             pltpu.VMEM((ny,) + column, F32),
-            pltpu.VMEM((nx,) + column, F32),
-            pltpu.VMEM((ny,) + column, F32),
-            pltpu.VMEM((nx,) + column, F32),
-            pltpu.VMEM((ny,) + column, F32),
+            pltpu.VMEM((nx, vectors // 2, size_z), F32),
+            pltpu.VMEM((ny, vectors // 2, size_z), F32),
+            pltpu.VMEM((nx, vectors // 2, size_z), F32),
+            pltpu.VMEM((ny, vectors // 2, size_z), F32),
+            pltpu.VMEM(flat, F32),
+            pltpu.VMEM(flat, F32),
+            pltpu.SemaphoreType.DMA((2,)),
             pltpu.SemaphoreType.DMA((8,)),
             pltpu.SemaphoreType.DMA((27,)),
             pltpu.SemaphoreType.DMA((27,)),

time: 45.5 us -> 44.6 us (0.980)
  Pallas kernels: 41.4 us -> 40.4 us
    pallas_call x1, Pallas kernels: 41.4 us -> 40.4 us  [per_device(): pl.pallas_call(functools.partial(kernel, nx, ny, scale), out_shape=[jax.S...]
where the time goes in v3:
time: 44.6 us; the launch traced here: 44.4 us
  Pallas kernels  40.4 us (91%)
  local copies, waits for them, and re-layouts  3.34 us (7%)
  between operations  0.65 us (1%)
    pallas_call x1, Pallas kernels, per_device(): pl.pallas_call(functools.partial(kernel, nx, ny, scale), out_shape=[jax.S...  40.4 us
    unnamed x7, local copies, waits for them, and re-layouts  3.34 us

profile of v3, /device:TPU:0, one launch (start us, length us, event | category | flops | bytes accessed | tf_op | source)
XLA Modules:
  0.0 44.4 jit_solution(9092509989923976176)
XLA Ops:
  0.6 40.4 %shard_map.103 = (f32[1024,128]{1,0:T(8,128)}, f32[1024,128]{1,0:T(8,128)}, f32[16,16]{1,0:T(8,128)}) custom-call(f32[1024,128]{1,0:T(8,128)} %bitcast.6, f32[1024,128]{1,0:T(8,128)} %bitcast.7, f32[8,8,128]{2,1,0:T(8,128)} %cond_hbm.1, f32[8,8,128]{2,1,0:T(8,128)} %diag_hbm.1, f32[13,8,8,128]{3,2,1,0:T(8,128)} %lower_hbm.1, s32[8,13]{1,0:T(8,128)} %pattern_hbm.1, ...), custom_call_target="tpu_custom_call" | custom-call | tf_op jit(solution)/shard_map/pallas_call | solution.py:507
  41.1 0.0 copy-start
  41.1 1.9 %copy.14 = f32[16,8,8,128]{3,2,1,0:T(8,128)} copy(f32[16,8,8,128]{3,2,1,0:T(8,128)} %bitcast.5) | data formatting | bytes 1048576
  43.0 0.0 copy-done
  43.0 0.0 copy-start.1
  43.0 0.8 %copy.15 = f32[16,8,8,128]{3,2,1,0:T(8,128)} copy(f32[16,8,8,128]{3,2,1,0:T(8,128)S(1)} %bitcast.4) | data formatting | bytes 1048576
  43.8 0.0 copy-done.1
  43.8 0.6 %copy.16 = f32[16,16]{1,0:T(8,128)} copy(f32[16,16]{1,0:T(8,128)S(1)} %copy-done.1) | data formatting | bytes 2048
Async XLA Ops:
  41.1 2.0 %copy-start = (f32[1024,128]{1,0:T(8,128)S(1)}, f32[1024,128]{1,0:T(8,128)}, u32[]{:S(2)}) copy-start(f32[1024,128]{1,0:T(8,128)} %get-tuple-element.7) | copy-start | bytes 1572868
  43.0 0.8 %copy-start.1 = (f32[16,16]{1,0:T(8,128)S(1)}, f32[16,16]{1,0:T(8,128)}, u32[]{:S(2)}) copy-start(f32[16,16]{1,0:T(8,128)} %get-tuple-element.14) | copy-start | bytes 3076
